TPU v7x, 256 devices: a whole 4x4x8 slice. The times are simulated.
256 devices in a mesh: ax: 2 (over core), rad: 16 (over y, x), span: 8 (over z).
Axes of the slice: x: 4, y: 4, z: 8, core: 2. Of those that a mesh axis runs over, the one named last changes fastest.
Arguments:
- tensor: float32 [1024, 64, 32, 128], P('ax', 'rad', 'span'), may hold values from -6 to 6
- radial_factor: float32 [64, 16], P('rad'), may hold values from -1 to 1
- span_factor: float32 [32, 16], P('span'), may hold values from -1.5 to 1.5
- start_factor: float32 [1024, 128], P('ax'), may hold values from -0.1875 to 0.1875
Outputs:
- core_block: float32 [128, 16, 16, 128], P(None, 'rad', 'span')
All inputs are finite; a program needn't handle non-finite values.
Results may differ from a plain program's by a relative error of at most 0.00015.
Values sent between devices are 32-bit elements; how exact they have to be, the bound alone decides.
A program may use at most 128 MiB of HBM per device.

v0:
```python
import jax
import jax.numpy as jnp
from jax import lax
from jax.sharding import PartitionSpec as P

RANK = 128
ITERS = 2


def body(tensor, radial_factor, span_factor, start_factor):
    highest = lax.Precision.HIGHEST
    radial_part = jnp.einsum("ijkr,jp->ipkr", tensor, radial_factor, precision=highest)
    radial_block = lax.psum_scatter(radial_part, "rad", scatter_dimension=1, tiled=True)
    span_part = jnp.einsum("ipkr,kq->ipqr", radial_block, span_factor, precision=highest)
    ttm_block = lax.psum_scatter(span_part, "span", scatter_dimension=2, tiled=True)
    local_rows = ttm_block.shape[0]
    unfolded = ttm_block.reshape(local_rows, -1)
    factor = start_factor
    for sweep_index in range(ITERS):
        small_matrix = lax.psum(jnp.einsum("ic,ia->ca", unfolded, factor, precision=highest), "ax")
        image_part = jnp.dot(unfolded, small_matrix, precision=highest)
        whole_images = lax.psum(image_part, ("rad", "span"))
        gram_matrix = lax.psum(jnp.dot(whole_images.T, whole_images, precision=highest), "ax")
        cholesky_factor = jnp.linalg.cholesky(gram_matrix)
        factor = jax.scipy.linalg.solve_triangular(cholesky_factor, whole_images.T, lower=True).T
    core_flat = lax.psum(jnp.einsum("ia,ic->ac", factor, unfolded, precision=highest), "ax")
    core_local = core_flat.reshape(RANK, ttm_block.shape[1], ttm_block.shape[2], ttm_block.shape[3])
    return core_local


def solution(mesh):
    in_specs = (P("ax", "rad", "span", None), P("rad", None), P("span", None), P("ax", None))
    out_specs = P(None, "rad", "span", None)
    return jax.shard_map(body, mesh=mesh, in_specs=in_specs, out_specs=out_specs, check_vma=False)
```

profile of v0, /device:TPU:1, one launch (start us, length us, event | category | flops | bytes accessed | tf_op | source)
XLA Modules:
  0.0 868.6 jit_solution(4356090178299347880)
XLA Ops:
  6.5 16.5 %convolution_bitcast_fusion = f32[512,16,4,128]{3,1,2,0:T(8,128)S(1)} fusion(f32[512,4,4,128]{3,2,1,0:T(4,128)} %param.7, f32[4,16]{1,0:T(4,128)} %param.8), kind=kOutput, calls=%fused_computation | convolution fusion | flops 201326592 | bytes 20971776 | tf_op jit(solution)/shard_map/ijkr,jp->ipkr/dot_general | solution.py:12
  23.0 11.8 %copy.21 = f32[512,16,4,128]{3,0,2,1:T(8,128)} copy(f32[512,16,4,128]{3,1,2,0:T(8,128)S(1)} %convolution_bitcast_fusion) | data formatting | bytes 33554432 | tf_op jit(solution)/shard_map/ijkr,jp->ipkr/transpose | solution.py:12
  34.8 0.0 reduce-scatter.7.cloned.1.call-update
  34.8 0.2 reduce-scatter.5.cloned.1.call-start
  35.0 119.0 %reduce-scatter.7.cloned.1.call-done = f32[512,1,4,128]{3,0,2,1:T(8,128)} async-done(((f32[512,16,4,128]{3,0,2,1:T(8,128)}), f32[512,1,4,128]{3,0,2,1:T(8,128)}) %reduce-scatter.7.cloned.1.call-update) | async-done | bytes 1048592
  154.1 5.1 convolution_bitcast_fusion.1
  159.1 3.2 copy.23
  162.4 0.0 reduce-scatter.5.cloned.1.call-update
  162.4 0.0 all-reduce.9.cloned.1.call-start
  162.4 55.4 %reduce-scatter.5.cloned.1.call-done = f32[512,1,2,128]{3,0,1,2:T(8,128)} async-done(((f32[512,1,16,128]{3,0,1,2:T(8,128)}), f32[512,1,2,128]{3,0,1,2:T(8,128)}) %reduce-scatter.5.cloned.1.call-update) | async-done | bytes 524304 | tf_op jit(solution)/shard_map/reduce_scatter | solution.py:15
  217.8 1.2 copy.24
  219.1 1.2 fusion.16
  220.3 0.0 all-reduce.9.cloned.1.call-update
  220.4 0.0 all-reduce.11.cloned.1.call-start
  220.4 28.1 %all-reduce.9.cloned.1.call-done = f32[256,128]{1,0:T(8,128)} async-done(((f32[256,128]{1,0:T(8,128)}), f32[256,128]{1,0:T(8,128)}) %all-reduce.9.cloned.1.call-update) | async-done | bytes 131088 | tf_op jit(solution)/shard_map/psum | solution.py:20
  248.5 2.6 fusion.17
  251.2 0.0 all-reduce.13.cloned.1.call-start
  251.2 211.5 %all-reduce.11.cloned.1.call-done = f32[512,128]{1,0:T(8,128)} async-done(((f32[512,128]{1,0:T(8,128)}), f32[512,128]{1,0:T(8,128)}) %all-reduce.11.cloned.1.call-update) | async-done | bytes 262160 | tf_op jit(solution)/shard_map/psum | solution.py:22
  462.7 2.2 fusion.18
  465.0 0.3 all-reduce.15.cloned.1.call-start
  465.3 31.2 %all-reduce.13.cloned.1.call-done = f32[128,128]{0,1:T(8,128)} async-done(((f32[128,128]{0,1:T(8,128)}), f32[128,128]{0,1:T(8,128)}) %all-reduce.13.cloned.1.call-update) | async-done | bytes 65552 | tf_op jit(solution)/shard_map/psum | solution.py:23
  496.5 0.9 copy.26
  497.4 0.9 fusion.11
  498.3 11.7 %cholesky.44 = f32[128,128]{1,0:T(8,128)S(1)} custom-call(f32[128,128]{1,0:T(8,128)S(1)} %fusion.11), custom_call_target="Cholesky" | custom-call | tf_op jit(solution)/shard_map/jit(cholesky)/cholesky | solution.py:24
  510.0 0.6 compare_reduce_fusion.1
  510.7 0.7 fusion.6
  511.3 9.8 %custom-call.6 = f32[1,128,128]{1,2,0:T(8,128)S(1)} custom-call(f32[1,128,128]{2,1,0:T(8,128)S(1)} %fusion.6), custom_call_target="InvertDiagBlocksLowerTriangular" | custom-call | tf_op jit(solution)/shard_map/jit(_solve_triangular)/triangular_solve | solution.py:25
  521.1 1.4 fusion.4
  522.5 1.2 fusion.19
  523.8 0.0 all-reduce.17.cloned.1.call-start
  523.8 30.1 %all-reduce.15.cloned.1.call-done = f32[256,128]{1,0:T(8,128)} async-done(((f32[256,128]{1,0:T(8,128)}), f32[256,128]{1,0:T(8,128)}) %all-reduce.15.cloned.1.call-update) | async-done | bytes 131088 | tf_op jit(solution)/shard_map/psum | solution.py:20
  553.9 2.6 fusion.20
  556.6 0.0 all-reduce.19.cloned.1.call-start
  556.6 212.6 %all-reduce.17.cloned.1.call-done = f32[512,128]{1,0:T(8,128)} async-done(((f32[512,128]{1,0:T(8,128)}), f32[512,128]{1,0:T(8,128)}) %all-reduce.17.cloned.1.call-update) | async-done | bytes 262160 | tf_op jit(solution)/shard_map/psum | solution.py:22
  769.2 2.2 fusion.21
  771.5 0.3 all-reduce.21.cloned.1.call-start
  771.8 31.2 %all-reduce.19.cloned.1.call-done = f32[128,128]{0,1:T(8,128)} async-done(((f32[128,128]{0,1:T(8,128)}), f32[128,128]{0,1:T(8,128)}) %all-reduce.19.cloned.1.call-update) | async-done | bytes 65552 | tf_op jit(solution)/shard_map/psum | solution.py:23
  802.9 0.9 copy.28
  803.9 0.9 fusion.9
  804.7 11.7 %cholesky.55 = f32[128,128]{1,0:T(8,128)S(1)} custom-call(f32[128,128]{1,0:T(8,128)S(1)} %fusion.9), custom_call_target="Cholesky" | custom-call | tf_op jit(solution)/shard_map/jit(cholesky)/cholesky | solution.py:24
  816.5 0.6 compare_reduce_fusion
  817.1 0.7 fusion.7
  817.8 9.8 %custom-call.7 = f32[1,128,128]{1,2,0:T(8,128)S(1)} custom-call(f32[1,128,128]{2,1,0:T(8,128)S(1)} %fusion.7), custom_call_target="InvertDiagBlocksLowerTriangular" | custom-call | tf_op jit(solution)/shard_map/jit(_solve_triangular)/triangular_solve | solution.py:25
  827.6 1.4 fusion.2
  829.0 0.7 fusion.22
  829.6 0.7 reshape.20
  830.4 30.2 %all-reduce.21.cloned.1.call-done = f32[128,1,2,128]{3,2,1,0:T(2,128)} async-done(((f32[128,1,2,128]{3,2,1,0:T(2,128)}), f32[128,1,2,128]{3,2,1,0:T(2,128)}) %all-reduce.21.cloned.1.call-update) | async-done | bytes 131088 | tf_op jit(solution)/shard_map/psum | solution.py:26
  860.5 1.6 copy.44
  (13 shorter events, 0.2 us)
Async XLA Ops:
  6.5 212.5 %copy-start = (f32[512,128]{1,0:T(8,128)S(1)}, f32[512,128]{1,0:T(8,128)}, u32[]{:S(2)}) copy-start(f32[512,128]{1,0:T(8,128)} %param.10) | copy-start | bytes 786436
  6.5 147.5 %reduce-scatter.7.cloned.1.call-start = ((), (), s32[]{:S(2)}) async-start(), calls=%async_computation.10 | async-start | bytes 17825792
  34.8 119.3 %copy-start.1 = (f32[4,16]{1,0:T(4,128)S(1)}, f32[4,16]{1,0:T(4,128)}, u32[]{:S(2)}) copy-start(f32[4,16]{1,0:T(4,128)} %param.9) | copy-start | bytes 772
  34.8 183.0 %reduce-scatter.5.cloned.1.call-start = ((), (), s32[]{:S(2)}) async-start(), calls=%async_computation.2 | async-start | bytes 4718592 | tf_op jit(solution)/shard_map/reduce_scatter | solution.py:15
  162.4 86.2 %all-reduce.9.cloned.1.call-start = ((), (), s32[]{:S(2)}) async-start(), calls=%async_computation.3 | async-start | bytes 262144 | tf_op jit(solution)/shard_map/psum | solution.py:20
  220.4 242.4 %all-reduce.11.cloned.1.call-start = ((), (), s32[]{:S(2)}) async-start(), calls=%async_computation.4 | async-start | bytes 524288 | tf_op jit(solution)/shard_map/psum | solution.py:22
  251.2 245.3 %all-reduce.13.cloned.1.call-start = ((), (), s32[]{:S(2)}) async-start(), calls=%async_computation.5 | async-start | bytes 131072 | tf_op jit(solution)/shard_map/psum | solution.py:23
  465.0 89.0 %all-reduce.15.cloned.1.call-start = ((), (), s32[]{:S(2)}) async-start(), calls=%async_computation.6 | async-start | bytes 262144 | tf_op jit(solution)/shard_map/psum | solution.py:20
  523.8 245.4 %all-reduce.17.cloned.1.call-start = ((), (), s32[]{:S(2)}) async-start(), calls=%async_computation.7 | async-start | bytes 524288 | tf_op jit(solution)/shard_map/psum | solution.py:22
  556.6 246.4 %all-reduce.19.cloned.1.call-start = ((), (), s32[]{:S(2)}) async-start(), calls=%async_computation.8 | async-start | bytes 131072 | tf_op jit(solution)/shard_map/psum | solution.py:23
  771.5 89.1 %all-reduce.21.cloned.1.call-start = ((), (), s32[]{:S(2)}) async-start(), calls=%async_computation.9 | async-start | bytes 262144 | tf_op jit(solution)/shard_map/psum | solution.py:26
Sparse Core Ops, SparseCore 0:
  34.9 119.0 reduce-scatter.6
  162.5 55.2 reduce-scatter.4
  220.5 28.0 all-reduce.8
  253.8 208.8 all-reduce.10
  465.3 31.1 all-reduce.12
  523.9 29.9 all-reduce.14
  560.2 208.9 all-reduce.16
  771.7 31.1 all-reduce.18
  830.5 30.0 all-reduce.20
where the time goes:
time: 869 us
  waiting for transfers between devices  749 us (86%)
  other arithmetic  47.4 us (5%)
  matrix products  37.1 us (4%)
  local copies, waits for them, and re-layouts  20.4 us (2%)
  between operations  13.3 us (2%)
    psum x2, waiting for transfers between devices, body(): whole_images = lax.psum(image_part, ('rad', 'span'))  424 us
    unnamed x10, waiting for transfers between devices  119 us
    psum x2, waiting for transfers between devices, body(): lax.psum(jnp.dot(whole_images.T, whole_images, precision=highest), 'ax')  62.4 us
    psum x2, waiting for transfers between devices, body(): lax.psum(jnp.einsum('ic,ia->ca', unfolded, factor, precision=highest), 'ax')  58.2 us
    reduce_scatter x1, waiting for transfers between devices, body(): lax.psum_scatter(span_part, 'span', scatter_dimension=2, tiled=True)  55.4 us
    psum x1, waiting for transfers between devices, body(): lax.psum(jnp.einsum('ia,ic->ac', factor, unfolded, precision=highest), 'ax')  30.2 us
    another operation x6, other arithmetic, body(): cholesky_factor = jnp.linalg.cholesky(gram_matrix)  24.8 us
    another operation x4, other arithmetic, body(): jax.scipy.linalg.solve_triangular(cholesky_factor, whole_images.T, lower=...  20.9 us
  transfers between devices with their start and end apart: 9, of which 9 were waited for; matrix products, arithmetic and copies ran while one was open for 0% of the time, Pallas kernels for 0%

commit v1 on v0

v1 whole, which is shorter than its diff:
```python
import functools

import jax
import jax.numpy as jnp
from jax import lax
from jax.experimental import pallas as pl
from jax.experimental.pallas import tpu as pltpu
from jax.sharding import PartitionSpec as P

MESH = pl.DeviceIdType.MESH
HIGHEST = lax.Precision.HIGHEST
LANES = 128
CHUNK = 8


def mm(a, b):
    return lax.dot_general(a, b, (((1,), (0,)), ((), ())), precision=HIGHEST, preferred_element_type=jnp.float32)


def mm_nt(a, b):
    return lax.dot_general(a, b, (((1,), (1,)), ((), ())), precision=HIGHEST, preferred_element_type=jnp.float32)


def mm_tn(a, b):
    return lax.dot_general(a, b, (((0,), (0,)), ((), ())), precision=HIGHEST, preferred_element_type=jnp.float32)


def iota(shape, dim):
    return lax.broadcasted_iota(jnp.int32, shape, dim)


def kernel(nr, nz, gx, t_ref, a_ref, b_ref, f_ref, out_ref,
           xb, ag, bg, ma, mb, ub, wb, ysend, yb, yt, f0t,
           sx, sr, part, r1, s1, r2, s2, im, gx_s, gr, ae, linv, cs, fr,
           own_sem, ab_send, ab_recv, t_send, t_recv, w_send, w_recv, y_send, y_recv,
           x_send, x_recv, g_send, g_recv, r1_send, r1_recv, r2_send, r2_recv, r3_send, r3_recv,
           f_send, f_recv):
    c = lax.axis_index("ax")
    m = lax.axis_index("rad")
    z = lax.axis_index("span")
    gy = nr // gx
    rj, rk = 2 * nz, nr
    il = f_ref.shape[0]
    bi = il // nr
    nc = bi // CHUNK
    my, mx = m // gx, m % gx

    def xy_peer(d):
        return ((my + d // gx) % gy) * gx + (mx + d % gx) % gx

    def z_peer(d):
        return (z + d) % nz

    def remote(src, dst, send, recv, dev):
        return pltpu.make_async_remote_copy(src_ref=src, dst_ref=dst, send_sem=send, recv_sem=recv, device_id=dev, device_id_type=MESH)

    def to_xy(src_of, dst, send, recv):
        @pl.loop(1, nr)
        def _(d):
            peer = xy_peer(d)
            remote(src_of(peer), dst, send, recv, (c, peer, z)).start()

    def to_z(src_of, dst, send, recv):
        @pl.loop(1, nz)
        def _(d):
            peer = z_peer(d)
            remote(src_of(peer), dst, send, recv, (c, m, peer)).start()

    def to_core(src, dst, send, recv):
        remote(src, dst, send, recv, (1 - c, m, z)).start()

    def wait(view, sem):
        pltpu.make_async_copy(view, view, sem).wait()

    dest_m, dest_z = 2 * z + c, m // 2
    src_c, src_z = m % 2, m // 2
    stays = jnp.logical_and(dest_m == m, dest_z == z)
    stays_here = jnp.logical_and(stays, src_c == c)

    barrier = pltpu.get_barrier_semaphore()

    def greet(dev):
        pl.semaphore_signal(barrier, inc=1, device_id=dev, device_id_type=MESH)

    @pl.loop(1, nr)
    def _(d):
        greet((c, xy_peer(d), z))

    @pl.loop(1, nz)
    def _(d):
        greet((c, m, z_peer(d)))

    greet((1 - c, m, z))
    for h in range(2):
        mine = jnp.logical_and(jnp.logical_and(src_c == c, 2 * z + h == m), src_z == z)

        @pl.when(jnp.logical_not(mine))
        def _():
            greet((src_c, 2 * z + h, src_z))

    ag[m] = jnp.zeros((8, LANES), jnp.float32)
    ag[m, 0:4, 0:rj] = a_ref[...]
    bg[z] = jnp.zeros((8, LANES), jnp.float32)
    bg[z, 0:4, 0:rk] = b_ref[...]
    pl.semaphore_wait(barrier, (nr - 1) + (nz - 1) + 1 + 2 - stays_here.astype(jnp.int32))

    to_xy(lambda p: ag.at[m], ag.at[m], ab_send.at[0], ab_recv.at[0])
    to_z(lambda p: bg.at[z], bg.at[z], ab_send.at[1], ab_recv.at[1])

    def t_rows(peer, k):
        return t_ref.at[pl.ds(pl.multiple_of((peer * bi + k * CHUNK) * 16, 128), CHUNK * 16), :]

    @pl.loop(0, nc)
    def _(k):
        pltpu.make_async_copy(t_rows(m, k), xb.at[k, m], own_sem.at[0, k]).start()
        to_xy(lambda p: t_rows(p, k), xb.at[k, m], t_send, t_recv.at[k])

    f0t[...] = f_ref[...].T

    wait(ag.at[pl.ds(0, nr - 1)], ab_recv.at[0])
    wait(bg.at[pl.ds(0, nz - 1)], ab_recv.at[1])

    rows, cols = rj * 4, nr * 16
    pick = (iota((rows, LANES), 0) // 4 == iota((rows, LANES), 1)).astype(jnp.float32)
    spread_row, spread_col = iota((nr * 8, cols), 0), iota((nr * 8, cols), 1)
    spread = (spread_row == (spread_col // 16) * 8 + (spread_col % 16) // 4).astype(jnp.float32)
    full = mm(mm_nt(pick, ag[...].reshape(nr * 8, LANES)), spread)
    ma[...] = jnp.where(iota((rows, cols), 0) % 4 == iota((rows, cols), 1) % 4, full, 0.0)

    rows, cols = rk * 16, nz * 64
    pick = (iota((rows, LANES), 0) // 16 == iota((rows, LANES), 1)).astype(jnp.float32)
    spread_row, spread_col = iota((nz * 8, cols), 0), iota((nz * 8, cols), 1)
    spread = (spread_row == (spread_col // 64) * 8 + spread_col % 4).astype(jnp.float32)
    full = mm(mm_nt(pick, bg[...].reshape(nz * 8, LANES)), spread)
    row, col = iota((rows, cols), 0), iota((rows, cols), 1)
    same = jnp.logical_and((row // 8) % 2 == (col // 4) % 2, row % 8 == (col // 8) % 8)
    mb[...] = jnp.where(same, full, 0.0)

    def radial(k):
        wait(xb.at[k, pl.ds(0, nr - 1)], t_recv.at[k])
        wait(xb.at[k, 0], own_sem.at[0, k])

        @pl.loop(0, CHUNK // 2)
        def _(h):
            at = pl.multiple_of(h * 32, 32)
            both = xb[k, :, pl.ds(at, 32), :]
            x0 = both[:, 0:16, :].reshape(nr * 16, LANES)
            x1 = both[:, 16:32, :].reshape(nr * 16, LANES)
            u = mm(ma[...], jnp.concatenate([x0, x1], axis=1))
            at8 = pl.multiple_of(h * 16, 16)
            ub[k, :, pl.ds(at8, 8), :] = u[:, 0:LANES].reshape(nz, 8, LANES)
            ub[k, :, pl.ds(at8 + 8, 8), :] = u[:, LANES:].reshape(nz, 8, LANES)

        pltpu.make_async_copy(ub.at[k, z], wb.at[k, z], own_sem.at[1, k]).start()
        to_z(lambda p: ub.at[k, p], wb.at[k, z], w_send, w_recv.at[k])

    def y_rows(k):
        return yb.at[:, pl.ds(pl.multiple_of(m * bi + k * CHUNK, 8), CHUNK), :]

    def span(k):
        wait(wb.at[k, pl.ds(0, nz - 1)], w_recv.at[k])
        wait(wb.at[k, 0], own_sem.at[1, k])
        y = mm(mb[...], wb[k].reshape(nz * 64, LANES))
        ysend[k] = y.reshape(nr, 2, CHUNK, LANES)
        pltpu.make_async_copy(ysend.at[k, m], y_rows(k), own_sem.at[2, k]).start()
        to_xy(lambda p: ysend.at[k, p], y_rows(k), y_send, y_recv)

    radial(0)

    @pl.loop(1, nc)
    def _(k):
        radial(k)
        span(k - 1)

    span(nc - 1)
    wait(yb.at[:, pl.ds(0, (nr - 1) * bi), :], y_recv)
    for k in range(nc):
        wait(ysend.at[0, 0], own_sem.at[2, k])

    def chol_start(gram):
        ae[:, 0:LANES] = gram
        eye = iota((LANES, LANES), 0) == iota((LANES, LANES), 1)
        ae[:, LANES:] = eye.astype(jnp.float32)

    sub = iota((8, LANES), 0)
    lane = iota((8, LANES), 1)

    def chol_blocks(lo, hi):
        @pl.loop(lo, hi)
        def _(b):
            at = pl.multiple_of(b * 8, 8)
            d = pltpu.roll(ae[pl.ds(at, 8), 0:LANES], (LANES - b * 8) % LANES, 1)
            e = ae[pl.ds(at, 8), LANES:]
            scale = jnp.zeros((8, LANES), jnp.float32)
            for t in range(8):
                column = jnp.broadcast_to(d[:, t:t + 1], (8, LANES))
                pivot = jnp.broadcast_to(column[t:t + 1, :], (8, LANES))
                f = jnp.where(sub > t, column / pivot, 0.0)
                scale = jnp.where(sub == t, lax.rsqrt(pivot), scale)
                d = d - f * jnp.broadcast_to(d[t:t + 1, :], (8, LANES))
                e = e - f * jnp.broadcast_to(e[t:t + 1, :], (8, LANES))
            d = pltpu.roll(d * scale, b * 8, 1)
            e = e * scale
            later = jnp.where(lane >= b * 8 + 8, d, 0.0)
            ae[...] -= mm_tn(later, jnp.concatenate([d, e], axis=1))
            ae[pl.ds(at, 8), LANES:] = e

    def exchange_begin(n):
        to_core(sx.at[n], sr.at[n], x_send.at[n], x_recv.at[n])

    def reduce_1(n):
        to_xy(lambda p: part.at[n, pl.ds(pl.multiple_of(p * bi, 8), bi), :], r1.at[n, m], r1_send.at[n], r1_recv.at[n])
        r1[n, m] = part[n, pl.ds(pl.multiple_of(m * bi, 8), bi), :]

    def reduce_2(n):
        wait(r1.at[n, pl.ds(0, nr - 1)], r1_recv.at[n])
        total = r1[n, 0]
        for k in range(1, nr):
            total = total + r1[n, k]
        s1[n] = total
        to_z(lambda p: s1.at[n], r2.at[n, z], r2_send.at[n], r2_recv.at[n])
        r2[n, z] = total

    def reduce_3(n):
        wait(r2.at[n, pl.ds(0, nz - 1)], r2_recv.at[n])
        total = r2[n, 0]
        for k in range(1, nz):
            total = total + r2[n, k]
        s2[n] = total
        mine = pl.ds(pl.multiple_of(m * bi, 8), bi)
        to_xy(lambda p: s2.at[n], im.at[n, mine, :], r3_send.at[n], r3_recv.at[n])
        im[n, mine, :] = total

    def reduce_end(n):
        wait(im.at[n, pl.ds(0, (nr - 1) * bi), :], r3_recv.at[n])

    for p in range(2):
        sx[0, p] = mm(f0t[...], yb[p])
    exchange_begin(0)
    wait(sr.at[0], x_recv.at[0])
    part[0] = mm_nt(yb[0], sx[0, 0] + sr[0, 0]) + mm_nt(yb[1], sx[0, 1] + sr[0, 1])
    reduce_1(0)
    yt[0] = yb[0].T
    reduce_2(0)
    yt[1] = yb[1].T
    reduce_3(0)
    reduce_end(0)

    for p in range(2):
        sx[1, p] = mm(yt[p], im[0])
    exchange_begin(1)
    gx_s[0] = mm(im[0].T, im[0])
    to_core(gx_s.at[0], gr.at[0], g_send.at[0], g_recv.at[0])
    wait(sr.at[1], x_recv.at[1])
    part[1] = mm(yb[0], sx[1, 0] + sr[1, 0]) + mm(yb[1], sx[1, 1] + sr[1, 1])
    reduce_1(1)
    blocks = LANES // 8
    wait(gr.at[0], g_recv.at[0])
    chol_start(gx_s[0] + gr[0])
    chol_blocks(0, 5)
    reduce_2(1)
    chol_blocks(5, 10)
    reduce_3(1)
    chol_blocks(10, blocks)
    linv[...] = ae[:, LANES:]
    reduce_end(1)
    images = mm_nt(im[1], linv[...])
    gx_s[1] = mm(images.T, images)
    to_core(gx_s.at[1], gr.at[1], g_send.at[1], g_recv.at[1])

    for p in range(2):
        sx[2, p] = mm(yt[p], images)
    to_core(sx.at[2, 1 - c], sr.at[2, 0], x_send.at[2], x_recv.at[2])
    wait(gr.at[1], g_recv.at[1])
    chol_start(gx_s[1] + gr[1])
    chol_blocks(0, 3)
    wait(sr.at[2, 0], x_recv.at[2])
    cs[...] = sx[2, c] + sr[2, 0]
    slot = m % 2
    for h in range(2):
        @pl.when(jnp.logical_and(stays, c == h))
        def _():
            pltpu.make_async_copy(cs, fr.at[slot], f_recv.at[slot]).start()

        @pl.when(jnp.logical_not(jnp.logical_and(stays, c == h)))
        def _():
            remote(cs, fr.at[slot], f_send.at[h], f_recv.at[slot], (h, dest_m, dest_z)).start()

    chol_blocks(3, blocks)
    for q in range(2):
        wait(fr.at[q], f_recv.at[q])
        out_ref[:, q, :] = mm_nt(ae[:, LANES:], fr[q])

    wait(ag.at[pl.ds(0, nr - 1)], ab_send.at[0])
    wait(bg.at[pl.ds(0, nz - 1)], ab_send.at[1])
    wait(xb.at[:, pl.ds(0, nr - 1)], t_send)
    wait(wb.at[:, pl.ds(0, nz - 1)], w_send)
    wait(ysend.at[:, pl.ds(0, nr - 1)], y_send)
    for n in range(2):
        wait(sr.at[n], x_send.at[n])
        wait(gr.at[n], g_send.at[n])
        wait(r1.at[n, pl.ds(0, nr - 1)], r1_send.at[n])
        wait(r2.at[n, pl.ds(0, nz - 1)], r2_send.at[n])
        wait(im.at[n, pl.ds(0, (nr - 1) * bi), :], r3_send.at[n])
    wait(sr.at[2, 0], x_send.at[2])
    for h in range(2):
        @pl.when(jnp.logical_not(jnp.logical_and(stays, c == h)))
        def _():
            wait(cs, f_send.at[h])


def solution(mesh):
    nr, nz = mesh.shape["rad"], mesh.shape["span"]
    gx = 1
    while gx * gx < nr:
        gx *= 2

    def body(tensor, radial_factor, span_factor, start_factor):
        il = start_factor.shape[0]
        bi = il // nr
        nc = bi // CHUNK
        f32 = jnp.float32
        dma = pltpu.SemaphoreType.DMA
        vm = lambda *s: pltpu.VMEM(s, f32)
        scratch = [
            vm(nc, nr, CHUNK * 16, LANES),
            vm(nr, 8, LANES), vm(nz, 8, LANES),
            vm(nz * 8, nr * 16), vm(nr * 16, nz * 64),
            vm(nc, nz, CHUNK * 8, LANES), vm(nc, nz, CHUNK * 8, LANES),
            vm(nc, nr, 2, CHUNK, LANES),
            vm(2, il, LANES), vm(2, LANES, il), vm(LANES, il),
            vm(3, 2, LANES, LANES), vm(3, 2, LANES, LANES),
            vm(2, il, LANES),
            vm(2, nr, bi, LANES), vm(2, bi, LANES),
            vm(2, nz, bi, LANES), vm(2, bi, LANES),
            vm(2, il, LANES),
            vm(2, LANES, LANES), vm(2, LANES, LANES),
            vm(LANES, 2 * LANES), vm(LANES, LANES),
            vm(LANES, LANES), vm(2, LANES, LANES),
            dma((3, nc)),
            dma((2,)), dma((2,)),
            dma, dma((nc,)),
            dma, dma((nc,)),
            dma, dma,
            dma((3,)), dma((3,)),
            dma((2,)), dma((2,)),
            dma((2,)), dma((2,)), dma((2,)), dma((2,)), dma((2,)), dma((2,)),
            dma((2,)), dma((2,)),
        ]
        rows = tensor.reshape(il * 16, LANES)
        vmem = pl.BlockSpec(memory_space=pltpu.VMEM)
        core = pl.pallas_call(
            functools.partial(kernel, nr, nz, gx),
            out_shape=jax.ShapeDtypeStruct((LANES, 2, LANES), f32),
            in_specs=[pl.BlockSpec(memory_space=pl.ANY), vmem, vmem, vmem],
            out_specs=vmem,
            scratch_shapes=scratch,
            compiler_params=pltpu.CompilerParams(collective_id=0, has_side_effects=True, vmem_limit_bytes=48 * 1024 * 1024),
        )(rows, radial_factor, span_factor, start_factor)
        return core.reshape(LANES, 1, 2, LANES)

    in_specs = (P("ax", "rad", "span", None), P("rad", None), P("span", None), P("ax", None))
    out_specs = P(None, "rad", "span", None)
    return jax.shard_map(body, mesh=mesh, in_specs=in_specs, out_specs=out_specs, check_vma=False)
```

time: 869 us -> 157 us (0.18)
  waiting for transfers between devices: 749 us -> 0 us
  Pallas kernels: 0 us -> 152 us
  other arithmetic: 47.4 us -> 0 us
  matrix products: 37.1 us -> 0 us
  local copies, waits for them, and re-layouts: 20.4 us -> 5.16 us
  between operations: 13.3 us -> 0.01 us
    psum x7 -> x0, waiting for transfers between devices: 575 us -> none  [the longest x2 424 us: body(): whole_images = lax.psum(image_part, ('rad', 'span'))]
    pallas_call x0 -> x1, Pallas kernels: none -> 152 us  [body(): pl.pallas_call(functools.partial(kernel, nr, nz, gx), out_shape=jax.Shape...]
    unnamed x10 -> x0, waiting for transfers between devices: 119 us -> none
    reduce_scatter x1 -> x0, waiting for transfers between devices: 55.4 us -> none  [body(): lax.psum_scatter(span_part, 'span', scatter_dimension=2, tiled=True)]
    another operation x10 -> x0, other arithmetic: 45.7 us -> none  [the longest x6 24.8 us: body(): cholesky_factor = jnp.linalg.cholesky(gram_matrix)]
    dot_general x9 -> x0, matrix products: 34.4 us -> none  [the longest x1 16.5 us: body(): jnp.einsum('ijkr,jp->ipkr', tensor, radial_factor, precision=highest)]
    transpose x2 -> x0, local copies, waits for them, and re-layouts: 15 us -> none  [the longest x1 11.8 us: body(): jnp.einsum('ijkr,jp->ipkr', tensor, radial_factor, precision=highest)]
  transfers between devices with their start and end apart: 9 -> 0, of which waited for: 9 -> 0; matrix products, arithmetic and copies ran while one was open for 0% -> 0% of each run, Pallas kernels for 0% -> 0%
where the time goes in v1:
time: 157 us
  Pallas kernels  152 us (97%)
  local copies, waits for them, and re-layouts  5.16 us (3%)
    pallas_call x1, Pallas kernels, body(): pl.pallas_call(functools.partial(kernel, nr, nz, gx), out_shape=jax.Shape...  152 us
    unnamed x9, local copies, waits for them, and re-layouts  5.16 us

profile of v1, /device:TPU:1, one launch (start us, length us, event | category | flops | bytes accessed | tf_op | source)
XLA Modules:
  0.0 156.7 jit_solution(17954692051998005945)
XLA Ops:
  0.0 0.0 copy-start
  0.0 2.2 %copy-done = f32[512,4,4,128]{3,2,1,0:T(4,128)S(1)} copy-done((f32[512,4,4,128]{3,2,1,0:T(4,128)S(1)}, f32[512,4,4,128]{3,2,1,0:T(4,128)}, u32[]{:S(2)}) %copy-start) | copy-done | bytes 4194328
  2.2 0.0 copy-start.1
  2.2 0.9 copy-done.1
  3.1 0.0 copy-start.2
  3.1 0.7 copy-done.2
  3.8 0.0 copy-start.3
  3.8 0.7 copy-done.3
  4.5 151.6 %shard_map.46 = f32[128,2,128]{2,1,0:T(2,128)S(1)} custom-call(f32[8192,128]{1,0:T(8,128)S(1)} %bitcast.4, f32[4,16]{1,0:T(4,128)S(1)} %copy-done.2, f32[4,16]{1,0:T(4,128)S(1)} %copy-done.3, f32[512,128]{1,0:T(8,128)S(1)} %copy-done.1), custom_call_target="tpu_custom_call" | custom-call | tf_op jit(solution)/shard_map/pallas_call | solution.py:352
  156.1 0.7 copy.7
Async XLA Ops:
  0.0 2.2 %copy-start = (f32[512,4,4,128]{3,2,1,0:T(4,128)S(1)}, f32[512,4,4,128]{3,2,1,0:T(4,128)}, u32[]{:S(2)}) copy-start(f32[512,4,4,128]{3,2,1,0:T(4,128)} %param.4) | copy-start | bytes 12582916
  2.2 0.9 copy-start.1
  3.1 0.7 copy-start.2
  3.8 0.7 copy-start.3

commit v2 on v1

--- a/solution.py
+++ b/solution.py
@@ -10,7 +10,9 @@
 MESH = pl.DeviceIdType.MESH
 HIGHEST = lax.Precision.HIGHEST
 LANES = 128
-CHUNK = 8
+CHUNK = 4
+GROUP = 8
+PIVOTS = 16
 
 
 def mm(a, b):
@@ -25,14 +27,29 @@
     return lax.dot_general(a, b, (((0,), (0,)), ((), ())), precision=HIGHEST, preferred_element_type=jnp.float32)
 
 
+def split3(x):
+    high = x.astype(jnp.bfloat16)
+    rest = x - high.astype(jnp.float32)
+    mid = rest.astype(jnp.bfloat16)
+    return high, mid, (rest - mid.astype(jnp.float32)).astype(jnp.bfloat16)
+
+
+def mm_tn_stacked(a, b):
+    ah, am, al = split3(a)
+    bh, bm, bl = split3(b)
+    left = jnp.concatenate([ah, ah, ah, am, am, al], axis=0)
+    right = jnp.concatenate([bh, bm, bl, bh, bm, bh], axis=0)
+    return lax.dot_general(left, right, (((0,), (0,)), ((), ())), preferred_element_type=jnp.float32)
+
+
 def iota(shape, dim):
     return lax.broadcasted_iota(jnp.int32, shape, dim)
 
 
 def kernel(nr, nz, gx, t_ref, a_ref, b_ref, f_ref, out_ref,
-           xb, ag, bg, ma, mb, ub, wb, ysend, yb, yt, f0t,
+           av, bv, fv, xb, ag, bg, ma, mb, ub, wb, ysend, yb, yt, f0t,
            sx, sr, part, r1, s1, r2, s2, im, gx_s, gr, ae, linv, cs, fr,
-           own_sem, ab_send, ab_recv, t_send, t_recv, w_send, w_recv, y_send, y_recv,
+           in_sem, own_sem, ab_send, ab_recv, t_send, t_recv, w_send, w_recv, y_send, y_recv,
            x_send, x_recv, g_send, g_recv, r1_send, r1_recv, r2_send, r2_recv, r3_send, r3_recv,
            f_send, f_recv):
     c = lax.axis_index("ax")
@@ -42,7 +59,7 @@
     rj, rk = 2 * nz, nr
     il = f_ref.shape[0]
     bi = il // nr
-    nc = bi // CHUNK
+    nc, ng, per = bi // CHUNK, bi // GROUP, GROUP // CHUNK
     my, mx = m // gx, m % gx
 
     def xy_peer(d):
@@ -72,11 +89,21 @@
     def wait(view, sem):
         pltpu.make_async_copy(view, view, sem).wait()
 
+    pending = []
+
+    def finish():
+        for view, sem in pending:
+            wait(view, sem)
+
     dest_m, dest_z = 2 * z + c, m // 2
     src_c, src_z = m % 2, m // 2
     stays = jnp.logical_and(dest_m == m, dest_z == z)
     stays_here = jnp.logical_and(stays, src_c == c)
 
+    arriving = [pltpu.make_async_copy(src, dst, in_sem.at[n]) for n, (src, dst) in enumerate(((a_ref, av), (b_ref, bv), (f_ref, fv)))]
+    for copy in arriving:
+        copy.start()
+
     barrier = pltpu.get_barrier_semaphore()
 
     def greet(dev):
@@ -98,24 +125,30 @@
         def _():
             greet((src_c, 2 * z + h, src_z))
 
+    arriving[0].wait()
+    arriving[1].wait()
     ag[m] = jnp.zeros((8, LANES), jnp.float32)
-    ag[m, 0:4, 0:rj] = a_ref[...]
+    ag[m, 0:4, 0:rj] = av[...]
     bg[z] = jnp.zeros((8, LANES), jnp.float32)
-    bg[z, 0:4, 0:rk] = b_ref[...]
+    bg[z, 0:4, 0:rk] = bv[...]
     pl.semaphore_wait(barrier, (nr - 1) + (nz - 1) + 1 + 2 - stays_here.astype(jnp.int32))
 
     to_xy(lambda p: ag.at[m], ag.at[m], ab_send.at[0], ab_recv.at[0])
+    pending.append((ag.at[pl.ds(0, nr - 1)], ab_send.at[0]))
     to_z(lambda p: bg.at[z], bg.at[z], ab_send.at[1], ab_recv.at[1])
+    pending.append((bg.at[pl.ds(0, nz - 1)], ab_send.at[1]))
 
     def t_rows(peer, k):
-        return t_ref.at[pl.ds(pl.multiple_of((peer * bi + k * CHUNK) * 16, 128), CHUNK * 16), :]
+        return t_ref.at[pl.ds(pl.multiple_of((peer * bi + k * CHUNK) * 16, 64), CHUNK * 16), :]
 
     @pl.loop(0, nc)
     def _(k):
         pltpu.make_async_copy(t_rows(m, k), xb.at[k, m], own_sem.at[0, k]).start()
         to_xy(lambda p: t_rows(p, k), xb.at[k, m], t_send, t_recv.at[k])
 
-    f0t[...] = f_ref[...].T
+    pending.append((xb.at[:, pl.ds(0, nr - 1)], t_send))
+    arriving[2].wait()
+    f0t[...] = fv[...].T
 
     wait(ag.at[pl.ds(0, nr - 1)], ab_recv.at[0])
     wait(bg.at[pl.ds(0, nz - 1)], ab_recv.at[1])
@@ -147,69 +180,92 @@
             x0 = both[:, 0:16, :].reshape(nr * 16, LANES)
             x1 = both[:, 16:32, :].reshape(nr * 16, LANES)
             u = mm(ma[...], jnp.concatenate([x0, x1], axis=1))
-            at8 = pl.multiple_of(h * 16, 16)
-            ub[k, :, pl.ds(at8, 8), :] = u[:, 0:LANES].reshape(nz, 8, LANES)
-            ub[k, :, pl.ds(at8 + 8, 8), :] = u[:, LANES:].reshape(nz, 8, LANES)
-
-        pltpu.make_async_copy(ub.at[k, z], wb.at[k, z], own_sem.at[1, k]).start()
-        to_z(lambda p: ub.at[k, p], wb.at[k, z], w_send, w_recv.at[k])
-
-    def y_rows(k):
-        return yb.at[:, pl.ds(pl.multiple_of(m * bi + k * CHUNK, 8), CHUNK), :]
-
-    def span(k):
-        wait(wb.at[k, pl.ds(0, nz - 1)], w_recv.at[k])
-        wait(wb.at[k, 0], own_sem.at[1, k])
-        y = mm(mb[...], wb[k].reshape(nz * 64, LANES))
-        ysend[k] = y.reshape(nr, 2, CHUNK, LANES)
-        pltpu.make_async_copy(ysend.at[k, m], y_rows(k), own_sem.at[2, k]).start()
-        to_xy(lambda p: ysend.at[k, p], y_rows(k), y_send, y_recv)
+            at8 = pl.multiple_of((k % per) * CHUNK * 8 + h * 16, 16)
+            ub[k // per, :, pl.ds(at8, 8), :] = u[:, 0:LANES].reshape(nz, 8, LANES)
+            ub[k // per, :, pl.ds(at8 + 8, 8), :] = u[:, LANES:].reshape(nz, 8, LANES)
+
+        g, half = k // per, pl.ds(pl.multiple_of((k % per) * CHUNK * 8, CHUNK * 8), CHUNK * 8)
+        pltpu.make_async_copy(ub.at[g, z, half], wb.at[g, z, half], own_sem.at[1, k]).start()
+        to_z(lambda p: ub.at[g, p, half], wb.at[g, z, half], w_send, w_recv.at[k])
+
+    def y_rows(g):
+        return yb.at[:, pl.ds(pl.multiple_of(m * bi + g * GROUP, 8), GROUP), :]
+
+    def span(g):
+        for h in range(per):
+            wait(wb.at[g, pl.ds(0, nz - 1), pl.ds(0, CHUNK * 8)], w_recv.at[g * per + h])
+            wait(wb.at[g, 0, pl.ds(0, CHUNK * 8)], own_sem.at[1, g * per + h])
+        y = mm(mb[...], wb[g].reshape(nz * 64, LANES))
+        ysend[g] = y.reshape(nr, 2, GROUP, LANES)
+        pltpu.make_async_copy(ysend.at[g, m], y_rows(g), own_sem.at[2, g]).start()
+        to_xy(lambda p: ysend.at[g, p], y_rows(g), y_send, y_recv)
 
     radial(0)
-
-    @pl.loop(1, nc)
-    def _(k):
-        radial(k)
-        span(k - 1)
-
-    span(nc - 1)
+    radial(1)
+
+    @pl.loop(1, ng)
+    def _(g):
+        radial(g * per)
+        span(g - 1)
+        radial(g * per + 1)
+
+    span(ng - 1)
+    pending.extend([(wb.at[:, pl.ds(0, nz - 1)], w_send), (ysend.at[:, pl.ds(0, nr - 1)], y_send)])
     wait(yb.at[:, pl.ds(0, (nr - 1) * bi), :], y_recv)
-    for k in range(nc):
-        wait(ysend.at[0, 0], own_sem.at[2, k])
+    for g in range(ng):
+        wait(ysend.at[0, 0], own_sem.at[2, g])
 
     def chol_start(gram):
         ae[:, 0:LANES] = gram
         eye = iota((LANES, LANES), 0) == iota((LANES, LANES), 1)
         ae[:, LANES:] = eye.astype(jnp.float32)
 
-    sub = iota((8, LANES), 0)
-    lane = iota((8, LANES), 1)
+    tiles = range(PIVOTS // 8)
+    sub = [iota((8, LANES), 0) + 8 * g for g in tiles]
+    lane = iota((PIVOTS, LANES), 1)
+
+    def over_rows(x, t):
+        return jnp.broadcast_to(x[t:t + 1, :], (8, LANES))
 
     def chol_blocks(lo, hi):
         @pl.loop(lo, hi)
         def _(b):
-            at = pl.multiple_of(b * 8, 8)
-            d = pltpu.roll(ae[pl.ds(at, 8), 0:LANES], (LANES - b * 8) % LANES, 1)
-            e = ae[pl.ds(at, 8), LANES:]
-            scale = jnp.zeros((8, LANES), jnp.float32)
-            for t in range(8):
-                column = jnp.broadcast_to(d[:, t:t + 1], (8, LANES))
-                pivot = jnp.broadcast_to(column[t:t + 1, :], (8, LANES))
-                f = jnp.where(sub > t, column / pivot, 0.0)
-                scale = jnp.where(sub == t, lax.rsqrt(pivot), scale)
-                d = d - f * jnp.broadcast_to(d[t:t + 1, :], (8, LANES))
-                e = e - f * jnp.broadcast_to(e[t:t + 1, :], (8, LANES))
-            d = pltpu.roll(d * scale, b * 8, 1)
-            e = e * scale
-            later = jnp.where(lane >= b * 8 + 8, d, 0.0)
-            ae[...] -= mm_tn(later, jnp.concatenate([d, e], axis=1))
-            ae[pl.ds(at, 8), LANES:] = e
+            at = pl.multiple_of(b * PIVOTS, PIVOTS)
+            turned = pltpu.roll(ae[pl.ds(at, PIVOTS), 0:LANES], (LANES - b * PIVOTS) % LANES, 1)
+            d = [turned[8 * g:8 * g + 8] for g in tiles]
+            e = [ae[pl.ds(at + 8 * g, 8), LANES:] for g in tiles]
+            cols = [[jnp.broadcast_to(d[g][:, t:t + 1], (8, LANES)) for g in tiles] for t in range(PIVOTS)]
+            scale = [jnp.zeros((8, LANES), jnp.float32) for g in tiles]
+            for t in range(PIVOTS):
+                g0, t0 = t // 8, t % 8
+                pivot = over_rows(cols[t][g0], t0)
+                r = pltpu.reciprocal(pivot, approx=True)
+                r = r * (2.0 - pivot * r)
+                r = r * (2.0 - pivot * r)
+                f = {g: cols[t][g] * r for g in tiles if g >= g0}
+                f[g0] = jnp.where(sub[g0] > t, f[g0], 0.0)
+                scale[g0] = jnp.where(sub[g0] == t, lax.rsqrt(pivot), scale[g0])
+                for u in range(t + 1, PIVOTS):
+                    row = over_rows(cols[u][g0], t0)
+                    for g in f:
+                        cols[u][g] = cols[u][g] - f[g] * row
+                d_row, e_row = over_rows(d[g0], t0), over_rows(e[g0], t0)
+                for g in f:
+                    d[g] = d[g] - f[g] * d_row
+                    e[g] = e[g] - f[g] * e_row
+            rows = pltpu.roll(jnp.concatenate([d[g] * scale[g] for g in tiles], axis=0), b * PIVOTS, 1)
+            inverse = jnp.concatenate([e[g] * scale[g] for g in tiles], axis=0)
+            later = jnp.where(lane >= b * PIVOTS + PIVOTS, rows, 0.0)
+            ae[...] -= mm_tn_stacked(later, jnp.concatenate([rows, inverse], axis=1))
+            ae[pl.ds(at, PIVOTS), LANES:] = inverse
 
     def exchange_begin(n):
         to_core(sx.at[n], sr.at[n], x_send.at[n], x_recv.at[n])
+        pending.append((sr.at[n], x_send.at[n]))
 
     def reduce_1(n):
         to_xy(lambda p: part.at[n, pl.ds(pl.multiple_of(p * bi, 8), bi), :], r1.at[n, m], r1_send.at[n], r1_recv.at[n])
+        pending.append((r1.at[n, pl.ds(0, nr - 1)], r1_send.at[n]))
         r1[n, m] = part[n, pl.ds(pl.multiple_of(m * bi, 8), bi), :]
 
     def reduce_2(n):
@@ -219,6 +275,7 @@
             total = total + r1[n, k]
         s1[n] = total
         to_z(lambda p: s1.at[n], r2.at[n, z], r2_send.at[n], r2_recv.at[n])
+        pending.append((r2.at[n, pl.ds(0, nz - 1)], r2_send.at[n]))
         r2[n, z] = total
 
     def reduce_3(n):
@@ -229,6 +286,7 @@
         s2[n] = total
         mine = pl.ds(pl.multiple_of(m * bi, 8), bi)
         to_xy(lambda p: s2.at[n], im.at[n, mine, :], r3_send.at[n], r3_recv.at[n])
+        pending.append((im.at[n, pl.ds(0, (nr - 1) * bi), :], r3_send.at[n]))
         im[n, mine, :] = total
 
     def reduce_end(n):
@@ -251,29 +309,32 @@
     exchange_begin(1)
     gx_s[0] = mm(im[0].T, im[0])
     to_core(gx_s.at[0], gr.at[0], g_send.at[0], g_recv.at[0])
+    pending.append((gr.at[0], g_send.at[0]))
     wait(sr.at[1], x_recv.at[1])
     part[1] = mm(yb[0], sx[1, 0] + sr[1, 0]) + mm(yb[1], sx[1, 1] + sr[1, 1])
     reduce_1(1)
-    blocks = LANES // 8
+    blocks = LANES // PIVOTS
     wait(gr.at[0], g_recv.at[0])
     chol_start(gx_s[0] + gr[0])
-    chol_blocks(0, 5)
+    chol_blocks(0, 3)
     reduce_2(1)
-    chol_blocks(5, 10)
+    chol_blocks(3, 6)
     reduce_3(1)
-    chol_blocks(10, blocks)
+    chol_blocks(6, blocks)
     linv[...] = ae[:, LANES:]
     reduce_end(1)
     images = mm_nt(im[1], linv[...])
     gx_s[1] = mm(images.T, images)
     to_core(gx_s.at[1], gr.at[1], g_send.at[1], g_recv.at[1])
+    pending.append((gr.at[1], g_send.at[1]))
 
     for p in range(2):
         sx[2, p] = mm(yt[p], images)
     to_core(sx.at[2, 1 - c], sr.at[2, 0], x_send.at[2], x_recv.at[2])
+    pending.append((sr.at[2, 0], x_send.at[2]))
     wait(gr.at[1], g_recv.at[1])
     chol_start(gx_s[1] + gr[1])
-    chol_blocks(0, 3)
+    chol_blocks(0, 2)
     wait(sr.at[2, 0], x_recv.at[2])
     cs[...] = sx[2, c] + sr[2, 0]
     slot = m % 2
@@ -286,23 +347,12 @@
         def _():
             remote(cs, fr.at[slot], f_send.at[h], f_recv.at[slot], (h, dest_m, dest_z)).start()
 
-    chol_blocks(3, blocks)
+    chol_blocks(2, blocks)
     for q in range(2):
         wait(fr.at[q], f_recv.at[q])
         out_ref[:, q, :] = mm_nt(ae[:, LANES:], fr[q])
 
-    wait(ag.at[pl.ds(0, nr - 1)], ab_send.at[0])
-    wait(bg.at[pl.ds(0, nz - 1)], ab_send.at[1])
-    wait(xb.at[:, pl.ds(0, nr - 1)], t_send)
-    wait(wb.at[:, pl.ds(0, nz - 1)], w_send)
-    wait(ysend.at[:, pl.ds(0, nr - 1)], y_send)
-    for n in range(2):
-        wait(sr.at[n], x_send.at[n])
-        wait(gr.at[n], g_send.at[n])
-        wait(r1.at[n, pl.ds(0, nr - 1)], r1_send.at[n])
-        wait(r2.at[n, pl.ds(0, nz - 1)], r2_send.at[n])
-        wait(im.at[n, pl.ds(0, (nr - 1) * bi), :], r3_send.at[n])
-    wait(sr.at[2, 0], x_send.at[2])
+    finish()
     for h in range(2):
         @pl.when(jnp.logical_not(jnp.logical_and(stays, c == h)))
         def _():
@@ -318,16 +368,17 @@
     def body(tensor, radial_factor, span_factor, start_factor):
         il = start_factor.shape[0]
         bi = il // nr
-        nc = bi // CHUNK
+        nc, ng = bi // CHUNK, bi // GROUP
         f32 = jnp.float32
         dma = pltpu.SemaphoreType.DMA
         vm = lambda *s: pltpu.VMEM(s, f32)
         scratch = [
+            vm(*radial_factor.shape), vm(*span_factor.shape), vm(*start_factor.shape),
             vm(nc, nr, CHUNK * 16, LANES),
             vm(nr, 8, LANES), vm(nz, 8, LANES),
             vm(nz * 8, nr * 16), vm(nr * 16, nz * 64),
-            vm(nc, nz, CHUNK * 8, LANES), vm(nc, nz, CHUNK * 8, LANES),
-            vm(nc, nr, 2, CHUNK, LANES),
+            vm(ng, nz, GROUP * 8, LANES), vm(ng, nz, GROUP * 8, LANES),
+            vm(ng, nr, 2, GROUP, LANES),
             vm(2, il, LANES), vm(2, LANES, il), vm(LANES, il),
             vm(3, 2, LANES, LANES), vm(3, 2, LANES, LANES),
             vm(2, il, LANES),
@@ -337,7 +388,7 @@
             vm(2, LANES, LANES), vm(2, LANES, LANES),
             vm(LANES, 2 * LANES), vm(LANES, LANES),
             vm(LANES, LANES), vm(2, LANES, LANES),
-            dma((3, nc)),
+            dma((3,)), dma((3, nc)),
             dma((2,)), dma((2,)),
             dma, dma((nc,)),
             dma, dma((nc,)),
@@ -348,14 +399,14 @@
             dma((2,)), dma((2,)),
         ]
         rows = tensor.reshape(il * 16, LANES)
-        vmem = pl.BlockSpec(memory_space=pltpu.VMEM)
+        hbm = pl.BlockSpec(memory_space=pltpu.HBM)
         core = pl.pallas_call(
             functools.partial(kernel, nr, nz, gx),
             out_shape=jax.ShapeDtypeStruct((LANES, 2, LANES), f32),
-            in_specs=[pl.BlockSpec(memory_space=pl.ANY), vmem, vmem, vmem],
-            out_specs=vmem,
+            in_specs=[hbm] * 4,
+            out_specs=pl.BlockSpec(memory_space=pltpu.VMEM),
             scratch_shapes=scratch,
-            compiler_params=pltpu.CompilerParams(collective_id=0, has_side_effects=True, vmem_limit_bytes=48 * 1024 * 1024),
+            compiler_params=pltpu.CompilerParams(collective_id=0, has_side_effects=True, vmem_limit_bytes=62 * 1024 * 1024),
         )(rows, radial_factor, span_factor, start_factor)
         return core.reshape(LANES, 1, 2, LANES)
 

time: 157 us -> 144 us (0.917)
  Pallas kernels: 152 us -> 142 us
  local copies, waits for them, and re-layouts: 5.16 us -> 1.57 us
    pallas_call x1, Pallas kernels: 152 us -> 142 us  [body(): pl.pallas_call(functools.partial(kernel, nr, nz, gx), out_shape=jax.Shape...]
    unnamed x9 -> x1, local copies, waits for them, and re-layouts: 5.16 us -> 1.57 us
where the time goes in v2:
time: 144 us; the launch traced here: 143 us
  Pallas kernels  142 us (99%)
  local copies, waits for them, and re-layouts  1.57 us (1%)
    pallas_call x1, Pallas kernels, body(): pl.pallas_call(functools.partial(kernel, nr, nz, gx), out_shape=jax.Shape...  142 us

profile of v2, /device:TPU:1, one launch (start us, length us, event | category | flops | bytes accessed | tf_op | source)
XLA Modules:
  0.0 143.4 jit_solution(10002883347267498031)
XLA Ops:
  0.0 141.8 %shard_map.46 = f32[128,2,128]{2,1,0:T(2,128)} custom-call(f32[8192,128]{1,0:T(8,128)} %bitcast.4, f32[4,16]{1,0:T(4,128)} %a_ref.1, f32[4,16]{1,0:T(4,128)} %b_ref.1, f32[512,128]{1,0:T(8,128)} %f_ref.1), custom_call_target="tpu_custom_call" | custom-call | tf_op jit(solution)/shard_map/pallas_call | solution.py:403
  141.9 1.6 %copy.7 = f32[128,1,2,128]{3,2,1,0:T(2,128)} copy(f32[128,1,2,128]{3,2,1,0:T(2,128)} %bitcast.5) | data formatting | bytes 262144

commit v3 on v2

--- a/solution.py
+++ b/solution.py
@@ -48,10 +48,10 @@
 
 def kernel(nr, nz, gx, t_ref, a_ref, b_ref, f_ref, out_ref,
            av, bv, fv, xb, ag, bg, ma, mb, ub, wb, ysend, yb, yt, f0t,
-           sx, sr, part, r1, s1, r2, s2, im, gx_s, gr, ae, linv, cs, fr,
+           sx, sr, part, r1, s1, r2, s2, im, gx_s, gr, ae, linv, ya, yo, yot,
            in_sem, own_sem, ab_send, ab_recv, t_send, t_recv, w_send, w_recv, y_send, y_recv,
            x_send, x_recv, g_send, g_recv, r1_send, r1_recv, r2_send, r2_recv, r3_send, r3_recv,
-           f_send, f_recv):
+           v_send, v_recv):
     c = lax.axis_index("ax")
     m = lax.axis_index("rad")
     z = lax.axis_index("span")
@@ -63,10 +63,10 @@
     my, mx = m // gx, m % gx
 
     def xy_peer(d):
-        return ((my + d // gx) % gy) * gx + (mx + d % gx) % gx
+        return lax.rem(my + lax.div(d, gx), gy) * gx + lax.rem(mx + lax.rem(d, gx), gx)
 
     def z_peer(d):
-        return (z + d) % nz
+        return lax.rem(z + d, nz)
 
     def remote(src, dst, send, recv, dev):
         return pltpu.make_async_remote_copy(src_ref=src, dst_ref=dst, send_sem=send, recv_sem=recv, device_id=dev, device_id_type=MESH)
@@ -95,11 +95,6 @@
         for view, sem in pending:
             wait(view, sem)
 
-    dest_m, dest_z = 2 * z + c, m // 2
-    src_c, src_z = m % 2, m // 2
-    stays = jnp.logical_and(dest_m == m, dest_z == z)
-    stays_here = jnp.logical_and(stays, src_c == c)
-
     arriving = [pltpu.make_async_copy(src, dst, in_sem.at[n]) for n, (src, dst) in enumerate(((a_ref, av), (b_ref, bv), (f_ref, fv)))]
     for copy in arriving:
         copy.start()
@@ -118,20 +113,13 @@
         greet((c, m, z_peer(d)))
 
     greet((1 - c, m, z))
-    for h in range(2):
-        mine = jnp.logical_and(jnp.logical_and(src_c == c, 2 * z + h == m), src_z == z)
-
-        @pl.when(jnp.logical_not(mine))
-        def _():
-            greet((src_c, 2 * z + h, src_z))
-
     arriving[0].wait()
     arriving[1].wait()
     ag[m] = jnp.zeros((8, LANES), jnp.float32)
     ag[m, 0:4, 0:rj] = av[...]
     bg[z] = jnp.zeros((8, LANES), jnp.float32)
     bg[z, 0:4, 0:rk] = bv[...]
-    pl.semaphore_wait(barrier, (nr - 1) + (nz - 1) + 1 + 2 - stays_here.astype(jnp.int32))
+    pl.semaphore_wait(barrier, (nr - 1) + (nz - 1) + 1)
 
     to_xy(lambda p: ag.at[m], ag.at[m], ab_send.at[0], ab_recv.at[0])
     pending.append((ag.at[pl.ds(0, nr - 1)], ab_send.at[0]))
@@ -199,6 +187,9 @@
         ysend[g] = y.reshape(nr, 2, GROUP, LANES)
         pltpu.make_async_copy(ysend.at[g, m], y_rows(g), own_sem.at[2, g]).start()
         to_xy(lambda p: ysend.at[g, p], y_rows(g), y_send, y_recv)
+        owned = ya.at[z, :, :, pl.ds(pl.multiple_of(g * GROUP, 8), GROUP), :]
+        pltpu.make_async_copy(ysend.at[g, pl.ds(2 * z, 2)], owned, own_sem.at[3, g]).start()
+        to_z(lambda p: ysend.at[g, pl.ds(2 * p, 2)], owned, v_send.at[0], v_recv.at[0])
 
     radial(0)
     radial(1)
@@ -210,7 +201,7 @@
         radial(g * per + 1)
 
     span(ng - 1)
-    pending.extend([(wb.at[:, pl.ds(0, nz - 1)], w_send), (ysend.at[:, pl.ds(0, nr - 1)], y_send)])
+    pending.extend([(wb.at[:, pl.ds(0, nz - 1)], w_send), (ysend.at[:, pl.ds(0, nr - 1)], y_send), (ya.at[pl.ds(0, nz - 1)], v_send.at[0])])
     wait(yb.at[:, pl.ds(0, (nr - 1) * bi), :], y_recv)
     for g in range(ng):
         wait(ysend.at[0, 0], own_sem.at[2, g])
@@ -240,7 +231,6 @@
                 g0, t0 = t // 8, t % 8
                 pivot = over_rows(cols[t][g0], t0)
                 r = pltpu.reciprocal(pivot, approx=True)
-                r = r * (2.0 - pivot * r)
                 r = r * (2.0 - pivot * r)
                 f = {g: cols[t][g] * r for g in tiles if g >= g0}
                 f[g0] = jnp.where(sub[g0] > t, f[g0], 0.0)
@@ -300,6 +290,13 @@
     reduce_1(0)
     yt[0] = yb[0].T
     reduce_2(0)
+    wait(ya.at[pl.ds(0, nz - 1)], v_recv.at[0])
+    for g in range(ng):
+        wait(ysend.at[0, pl.ds(0, 2)], own_sem.at[3, g])
+    owned = yo.at[:, pl.ds(pl.multiple_of(m * bi, 8), bi), :]
+    pltpu.make_async_copy(ya.at[m // 2, :, m % 2], owned, in_sem.at[3]).start()
+    to_xy(lambda p: ya.at[p // 2, :, p % 2], owned, v_send.at[1], v_recv.at[1])
+    pending.append((yo.at[:, pl.ds(0, (nr - 1) * bi), :], v_send.at[1]))
     yt[1] = yb[1].T
     reduce_3(0)
     reduce_end(0)
@@ -318,6 +315,10 @@
     chol_start(gx_s[0] + gr[0])
     chol_blocks(0, 3)
     reduce_2(1)
+    wait(yo.at[:, pl.ds(0, (nr - 1) * bi), :], v_recv.at[1])
+    wait(ya.at[0, :, 0], in_sem.at[3])
+    for q in range(2):
+        yot[q] = yo[q].T
     chol_blocks(3, 6)
     reduce_3(1)
     chol_blocks(6, blocks)
@@ -328,35 +329,16 @@
     to_core(gx_s.at[1], gr.at[1], g_send.at[1], g_recv.at[1])
     pending.append((gr.at[1], g_send.at[1]))
 
-    for p in range(2):
-        sx[2, p] = mm(yt[p], images)
-    to_core(sx.at[2, 1 - c], sr.at[2, 0], x_send.at[2], x_recv.at[2])
-    pending.append((sr.at[2, 0], x_send.at[2]))
+    for q in range(2):
+        sx[2, q] = mm(yot[q], images)
+    exchange_begin(2)
     wait(gr.at[1], g_recv.at[1])
     chol_start(gx_s[1] + gr[1])
-    chol_blocks(0, 2)
-    wait(sr.at[2, 0], x_recv.at[2])
-    cs[...] = sx[2, c] + sr[2, 0]
-    slot = m % 2
-    for h in range(2):
-        @pl.when(jnp.logical_and(stays, c == h))
-        def _():
-            pltpu.make_async_copy(cs, fr.at[slot], f_recv.at[slot]).start()
-
-        @pl.when(jnp.logical_not(jnp.logical_and(stays, c == h)))
-        def _():
-            remote(cs, fr.at[slot], f_send.at[h], f_recv.at[slot], (h, dest_m, dest_z)).start()
-
-    chol_blocks(2, blocks)
+    chol_blocks(0, blocks)
+    wait(sr.at[2], x_recv.at[2])
     for q in range(2):
-        wait(fr.at[q], f_recv.at[q])
-        out_ref[:, q, :] = mm_nt(ae[:, LANES:], fr[q])
-
+        out_ref[:, q, :] = mm_nt(ae[:, LANES:], sx[2, q] + sr[2, q])
     finish()
-    for h in range(2):
-        @pl.when(jnp.logical_not(jnp.logical_and(stays, c == h)))
-        def _():
-            wait(cs, f_send.at[h])
 
 
 def solution(mesh):
@@ -387,8 +369,8 @@
             vm(2, il, LANES),
             vm(2, LANES, LANES), vm(2, LANES, LANES),
             vm(LANES, 2 * LANES), vm(LANES, LANES),
-            vm(LANES, LANES), vm(2, LANES, LANES),
-            dma((3,)), dma((3, nc)),
+            vm(nz, 2, 2, bi, LANES), vm(2, il, LANES), vm(2, LANES, il),
+            dma((4,)), dma((4, nc)),
             dma((2,)), dma((2,)),
             dma, dma((nc,)),
             dma, dma((nc,)),

time: 144 us -> 126 us (0.88)
  Pallas kernels: 142 us -> 125 us
    pallas_call x1, Pallas kernels: 142 us -> 125 us  [body(): pl.pallas_call(functools.partial(kernel, nr, nz, gx), out_shape=jax.Shape...]
where the time goes in v3:
time: 126 us
  Pallas kernels  125 us (99%)
  local copies, waits for them, and re-layouts  1.57 us (1%)
    pallas_call x1, Pallas kernels, body(): pl.pallas_call(functools.partial(kernel, nr, nz, gx), out_shape=jax.Shape...  125 us

profile of v3, /device:TPU:1, one launch (start us, length us, event | category | flops | bytes accessed | tf_op | source)
XLA Modules:
  0.0 126.3 jit_solution(9067870965231609587)
XLA Ops:
  0.0 124.8 %shard_map.46 = f32[128,2,128]{2,1,0:T(2,128)} custom-call(f32[8192,128]{1,0:T(8,128)} %bitcast.4, f32[4,16]{1,0:T(4,128)} %a_ref.1, f32[4,16]{1,0:T(4,128)} %b_ref.1, f32[512,128]{1,0:T(8,128)} %f_ref.1), custom_call_target="tpu_custom_call" | custom-call | tf_op jit(solution)/shard_map/pallas_call | solution.py:385
  124.8 1.6 %copy.7 = f32[128,1,2,128]{3,2,1,0:T(2,128)} copy(f32[128,1,2,128]{3,2,1,0:T(2,128)} %bitcast.5) | data formatting | bytes 262144

commit v4 on v3

--- a/solution.py
+++ b/solution.py
@@ -62,25 +62,23 @@
     nc, ng, per = bi // CHUNK, bi // GROUP, GROUP // CHUNK
     my, mx = m // gx, m % gx
 
-    def xy_peer(d):
-        return lax.rem(my + lax.div(d, gx), gy) * gx + lax.rem(mx + lax.rem(d, gx), gx)
-
-    def z_peer(d):
-        return lax.rem(z + d, nz)
+    xs = [lax.rem(mx + d, gx) for d in range(gx)]
+    ys = [lax.rem(my + d, gy) * gx for d in range(gy)]
+    steps = [(dy, dx) for dy in range(gy) for dx in range(gx) if dy or dx]
+    near_first = [ys[dy] + xs[dx] for dy, dx in steps]
+    steps.sort(key=lambda s: -min(s[0], gy - s[0]) - min(s[1], gx - s[1]))
+    xy_peers = [ys[dy] + xs[dx] for dy, dx in steps]
+    z_peers = [lax.rem(z + d, nz) for d in sorted(range(1, nz), key=lambda d: -min(d, nz - d))]
 
     def remote(src, dst, send, recv, dev):
         return pltpu.make_async_remote_copy(src_ref=src, dst_ref=dst, send_sem=send, recv_sem=recv, device_id=dev, device_id_type=MESH)
 
-    def to_xy(src_of, dst, send, recv):
-        @pl.loop(1, nr)
-        def _(d):
-            peer = xy_peer(d)
+    def to_xy(src_of, dst, send, recv, peers=xy_peers):
+        for peer in peers:
             remote(src_of(peer), dst, send, recv, (c, peer, z)).start()
 
     def to_z(src_of, dst, send, recv):
-        @pl.loop(1, nz)
-        def _(d):
-            peer = z_peer(d)
+        for peer in z_peers:
             remote(src_of(peer), dst, send, recv, (c, m, peer)).start()
 
     def to_core(src, dst, send, recv):
@@ -104,14 +102,10 @@
     def greet(dev):
         pl.semaphore_signal(barrier, inc=1, device_id=dev, device_id_type=MESH)
 
-    @pl.loop(1, nr)
-    def _(d):
-        greet((c, xy_peer(d), z))
-
-    @pl.loop(1, nz)
-    def _(d):
-        greet((c, m, z_peer(d)))
-
+    for peer in xy_peers:
+        greet((c, peer, z))
+    for peer in z_peers:
+        greet((c, m, peer))
     greet((1 - c, m, z))
     arriving[0].wait()
     arriving[1].wait()
@@ -132,7 +126,7 @@
     @pl.loop(0, nc)
     def _(k):
         pltpu.make_async_copy(t_rows(m, k), xb.at[k, m], own_sem.at[0, k]).start()
-        to_xy(lambda p: t_rows(p, k), xb.at[k, m], t_send, t_recv.at[k])
+        to_xy(lambda p: t_rows(p, k), xb.at[k, m], t_send, t_recv.at[k], near_first)
 
     pending.append((xb.at[:, pl.ds(0, nr - 1)], t_send))
     arriving[2].wait()
@@ -282,11 +276,15 @@
     def reduce_end(n):
         wait(im.at[n, pl.ds(0, (nr - 1) * bi), :], r3_recv.at[n])
 
+    def unfolded():
+        return jnp.concatenate([yb[0], yb[1]], axis=1)
+
+    both = mm(f0t[...], unfolded())
     for p in range(2):
-        sx[0, p] = mm(f0t[...], yb[p])
+        sx[0, p] = both[:, p * LANES:(p + 1) * LANES]
     exchange_begin(0)
     wait(sr.at[0], x_recv.at[0])
-    part[0] = mm_nt(yb[0], sx[0, 0] + sr[0, 0]) + mm_nt(yb[1], sx[0, 1] + sr[0, 1])
+    part[0] = mm_nt(unfolded(), jnp.concatenate([sx[0, p] + sr[0, p] for p in range(2)], axis=1))
     reduce_1(0)
     yt[0] = yb[0].T
     reduce_2(0)
@@ -301,14 +299,13 @@
     reduce_3(0)
     reduce_end(0)
 
-    for p in range(2):
-        sx[1, p] = mm(yt[p], im[0])
+    sx[1] = mm(yt[...].reshape(2 * LANES, il), im[0]).reshape(2, LANES, LANES)
     exchange_begin(1)
-    gx_s[0] = mm(im[0].T, im[0])
+    gx_s[0] = mm_tn(im[0], im[0])
     to_core(gx_s.at[0], gr.at[0], g_send.at[0], g_recv.at[0])
     pending.append((gr.at[0], g_send.at[0]))
     wait(sr.at[1], x_recv.at[1])
-    part[1] = mm(yb[0], sx[1, 0] + sr[1, 0]) + mm(yb[1], sx[1, 1] + sr[1, 1])
+    part[1] = mm(unfolded(), (sx[1] + sr[1]).reshape(2 * LANES, LANES))
     reduce_1(1)
     blocks = LANES // PIVOTS
     wait(gr.at[0], g_recv.at[0])
@@ -325,12 +322,11 @@
     linv[...] = ae[:, LANES:]
     reduce_end(1)
     images = mm_nt(im[1], linv[...])
-    gx_s[1] = mm(images.T, images)
+    gx_s[1] = mm_tn(images, images)
     to_core(gx_s.at[1], gr.at[1], g_send.at[1], g_recv.at[1])
     pending.append((gr.at[1], g_send.at[1]))
 
-    for q in range(2):
-        sx[2, q] = mm(yot[q], images)
+    sx[2] = mm(yot[...].reshape(2 * LANES, il), images).reshape(2, LANES, LANES)
     exchange_begin(2)
     wait(gr.at[1], g_recv.at[1])
     chol_start(gx_s[1] + gr[1])

time: 126 us -> 122 us (0.968)
  Pallas kernels: 125 us -> 120 us
    pallas_call x1, Pallas kernels: 125 us -> 120 us  [body(): pl.pallas_call(functools.partial(kernel, nr, nz, gx), out_shape=jax.Shape...]
where the time goes in v4:
time: 122 us
  Pallas kernels  120 us (98%)
  local copies, waits for them, and re-layouts  1.57 us (1%)
    pallas_call x1, Pallas kernels, body(): pl.pallas_call(functools.partial(kernel, nr, nz, gx), out_shape=jax.Shape...  120 us

profile of v4, /device:TPU:1, one launch (start us, length us, event | category | flops | bytes accessed | tf_op | source)
XLA Modules:
  0.0 122.1 jit_solution(12669545029427596014)
XLA Ops:
  0.0 120.5 %shard_map.46 = f32[128,2,128]{2,1,0:T(2,128)} custom-call(f32[8192,128]{1,0:T(8,128)} %bitcast.4, f32[4,16]{1,0:T(4,128)} %a_ref.1, f32[4,16]{1,0:T(4,128)} %b_ref.1, f32[512,128]{1,0:T(8,128)} %f_ref.1), custom_call_target="tpu_custom_call" | custom-call | tf_op jit(solution)/shard_map/pallas_call | solution.py:381
  120.5 1.6 %copy.7 = f32[128,1,2,128]{3,2,1,0:T(2,128)} copy(f32[128,1,2,128]{3,2,1,0:T(2,128)} %bitcast.5) | data formatting | bytes 262144

commit v5 on v4

--- a/solution.py
+++ b/solution.py
@@ -48,10 +48,11 @@
 
 def kernel(nr, nz, gx, t_ref, a_ref, b_ref, f_ref, out_ref,
            av, bv, fv, xb, ag, bg, ma, mb, ub, wb, ysend, yb, yt, f0t,
-           sx, sr, part, r1, s1, r2, s2, im, gx_s, gr, ae, linv, ya, yo, yot,
+           sx, sr, part, r1, s1, r2, s2, im, gx_s, gr, ae, linv, ya, yo, yd,
+           xz, zm, rm, vs, vr, yz,
            in_sem, own_sem, ab_send, ab_recv, t_send, t_recv, w_send, w_recv, y_send, y_recv,
            x_send, x_recv, g_send, g_recv, r1_send, r1_recv, r2_send, r2_recv, r3_send, r3_recv,
-           v_send, v_recv):
+           v_send, v_recv, q_send, q_recv, u_recv):
     c = lax.axis_index("ax")
     m = lax.axis_index("rad")
     z = lax.axis_index("span")
@@ -59,7 +60,9 @@
     rj, rk = 2 * nz, nr
     il = f_ref.shape[0]
     bi = il // nr
-    nc, ng, per = bi // CHUNK, bi // GROUP, GROUP // CHUNK
+    pb = bi - bi // 4
+    zb = (il - nr * pb) // nz
+    nc, ng, per, nq = pb // CHUNK, pb // GROUP, GROUP // CHUNK, zb // CHUNK
     my, mx = m // gx, m % gx
 
     xs = [lax.rem(mx + d, gx) for d in range(gx)]
@@ -121,35 +124,47 @@
     pending.append((bg.at[pl.ds(0, nz - 1)], ab_send.at[1]))
 
     def t_rows(peer, k):
-        return t_ref.at[pl.ds(pl.multiple_of((peer * bi + k * CHUNK) * 16, 64), CHUNK * 16), :]
-
-    @pl.loop(0, nc)
-    def _(k):
+        return t_ref.at[pl.ds(pl.multiple_of((peer * pb + k * CHUNK) * 16, 64), CHUNK * 16), :]
+
+    def t_ring(peer, k):
+        return t_ref.at[pl.ds(pl.multiple_of((nr * pb + peer * zb + k * CHUNK) * 16, 64), CHUNK * 16), :]
+
+    def to_plane(k):
         pltpu.make_async_copy(t_rows(m, k), xb.at[k, m], own_sem.at[0, k]).start()
         to_xy(lambda p: t_rows(p, k), xb.at[k, m], t_send, t_recv.at[k], near_first)
 
+    @pl.loop(0, nq)
+    def _(k):
+        pltpu.make_async_copy(t_ring(z, k), xz.at[k, z], own_sem.at[4, k]).start()
+        to_z(lambda p: t_ring(p, k), xz.at[k, z], q_send.at[0], q_recv.at[k])
+        to_plane(k)
+
+    @pl.loop(nq, nc)
+    def _(k):
+        to_plane(k)
+
     pending.append((xb.at[:, pl.ds(0, nr - 1)], t_send))
+    pending.append((xz.at[:, pl.ds(0, nz - 1)], q_send.at[0]))
     arriving[2].wait()
     f0t[...] = fv[...].T
 
     wait(ag.at[pl.ds(0, nr - 1)], ab_recv.at[0])
     wait(bg.at[pl.ds(0, nz - 1)], ab_recv.at[1])
 
-    rows, cols = rj * 4, nr * 16
-    pick = (iota((rows, LANES), 0) // 4 == iota((rows, LANES), 1)).astype(jnp.float32)
-    spread_row, spread_col = iota((nr * 8, cols), 0), iota((nr * 8, cols), 1)
-    spread = (spread_row == (spread_col // 16) * 8 + (spread_col % 16) // 4).astype(jnp.float32)
-    full = mm(mm_nt(pick, ag[...].reshape(nr * 8, LANES)), spread)
-    ma[...] = jnp.where(iota((rows, cols), 0) % 4 == iota((rows, cols), 1) % 4, full, 0.0)
-
-    rows, cols = rk * 16, nz * 64
-    pick = (iota((rows, LANES), 0) // 16 == iota((rows, LANES), 1)).astype(jnp.float32)
-    spread_row, spread_col = iota((nz * 8, cols), 0), iota((nz * 8, cols), 1)
-    spread = (spread_row == (spread_col // 64) * 8 + spread_col % 4).astype(jnp.float32)
-    full = mm(mm_nt(pick, bg[...].reshape(nz * 8, LANES)), spread)
-    row, col = iota((rows, cols), 0), iota((rows, cols), 1)
-    same = jnp.logical_and((row // 8) % 2 == (col // 4) % 2, row % 8 == (col // 8) % 8)
-    mb[...] = jnp.where(same, full, 0.0)
+    def spread(gathered, shape, row_div, col_div, col_of, same):
+        rows, cols = shape
+        n = gathered.shape[0] * 8
+        pick = (iota((rows, LANES), 0) // row_div == iota((rows, LANES), 1)).astype(jnp.float32)
+        at, col = iota((n, cols), 0), iota((n, cols), 1)
+        place = (at == (col // col_div) * 8 + col_of(col)).astype(jnp.float32)
+        full = mm(mm_nt(pick, gathered[...].reshape(n, LANES)), place)
+        return jnp.where(same(iota(shape, 0), iota(shape, 1)), full, 0.0)
+
+    ma[...] = spread(ag, ma.shape, 4, 16, lambda col: (col % 16) // 4, lambda r, col: r % 4 == col % 4)
+    mb[...] = spread(bg, mb.shape, 16, 64, lambda col: col % 4, lambda r, col: jnp.logical_and(
+        (r // 8) % 2 == (col // 4) % 2, r % 8 == (col // 8) % 8))
+    zm[...] = spread(bg, zm.shape, 8, 32, lambda col: col % 4, lambda r, col: r % 8 == (col // 4) % 8)
+    rm[...] = spread(ag, rm.shape, 8, 32, lambda col: col % 4, lambda r, col: r % 8 == (col // 4) % 8)
 
     def radial(k):
         wait(xb.at[k, pl.ds(0, nr - 1)], t_recv.at[k])
@@ -171,7 +186,7 @@
         to_z(lambda p: ub.at[g, p, half], wb.at[g, z, half], w_send, w_recv.at[k])
 
     def y_rows(g):
-        return yb.at[:, pl.ds(pl.multiple_of(m * bi + g * GROUP, 8), GROUP), :]
+        return yb.at[:, pl.ds(pl.multiple_of(m * pb + g * GROUP, 8), GROUP), :]
 
     def span(g):
         for h in range(per):
@@ -181,24 +196,87 @@
         ysend[g] = y.reshape(nr, 2, GROUP, LANES)
         pltpu.make_async_copy(ysend.at[g, m], y_rows(g), own_sem.at[2, g]).start()
         to_xy(lambda p: ysend.at[g, p], y_rows(g), y_send, y_recv)
-        owned = ya.at[z, :, :, pl.ds(pl.multiple_of(g * GROUP, 8), GROUP), :]
+
+    def ring_span(k):
+        wait(xz.at[k, pl.ds(0, nz - 1)], q_recv.at[k])
+        wait(xz.at[k, 0], own_sem.at[4, k])
+        for h in range(CHUNK // 2):
+            rows = xz[k, :, pl.ds(h * 32, 32), :].reshape(nz * 32, LANES)
+            vs[:, pl.ds((k * 2 + h) * 8, 8), :] = mm(zm[...], rows).reshape(nr, 8, LANES)
+        if k % per == per - 1:
+            rows = pl.ds((k // per) * GROUP * 4, GROUP * 4)
+            pltpu.make_async_copy(vs.at[m, rows], vr.at[m, rows], own_sem.at[5, k // per]).start()
+            to_xy(lambda p: vs.at[p, rows], vr.at[m, rows], q_send.at[1], u_recv.at[k // per])
+
+    def ring_y(g):
+        return yb.at[:, pl.ds(pl.multiple_of(nr * pb + z * zb + g * GROUP, 8), GROUP), :]
+
+    def ring_radial(g):
+        rows, part_rows = pl.ds(g * GROUP * 4, GROUP * 4), pl.ds(g * GROUP, GROUP)
+        wait(vr.at[pl.ds(0, nr - 1), rows], u_recv.at[g])
+        wait(vr.at[0, rows], own_sem.at[5, g])
+        y = mm(rm[...], vr[:, rows, :].reshape(nr * 32, LANES))
+        yz[:, part_rows, :] = y.reshape(rj, GROUP, LANES)
+        pltpu.make_async_copy(yz.at[pl.ds(2 * z, 2), part_rows], ring_y(g), own_sem.at[6, g]).start()
+        to_z(lambda p: yz.at[pl.ds(2 * p, 2), part_rows], ring_y(g), q_send.at[2], q_recv.at[nq])
+
+    radial(0)
+    radial(1)
+    ring_span(0)
+    radial(2)
+    span(0)
+    ring_span(1)
+    radial(3)
+    ring_span(2)
+    radial(4)
+    span(1)
+    ring_span(3)
+    radial(5)
+    ring_radial(0)
+    span(2)
+    ring_radial(1)
+    pending.extend([(wb.at[:, pl.ds(0, nz - 1)], w_send), (ysend.at[:, pl.ds(0, nr - 1)], y_send)])
+    pending.extend([(vr.at[pl.ds(0, nr - 1)], q_send.at[1]), (yb.at[:, pl.ds(0, (nz - 1) * zb), :], q_send.at[2])])
+    wait(yb.at[:, pl.ds(0, (nr - 1) * pb), :], y_recv)
+    wait(yb.at[:, pl.ds(0, (nz - 1) * zb), :], q_recv.at[nq])
+    for g in range(ng):
+        wait(ysend.at[0, 0], own_sem.at[2, g])
+    for g in range(zb // GROUP):
+        wait(yz.at[pl.ds(0, 2), pl.ds(0, GROUP)], own_sem.at[6, g])
+
+    def owned_z(g):
+        owned = ya.at[z, :, :, pl.ds(g * GROUP, GROUP), :]
         pltpu.make_async_copy(ysend.at[g, pl.ds(2 * z, 2)], owned, own_sem.at[3, g]).start()
         to_z(lambda p: ysend.at[g, pl.ds(2 * p, 2)], owned, v_send.at[0], v_recv.at[0])
 
-    radial(0)
-    radial(1)
-
-    @pl.loop(1, ng)
-    def _(g):
-        radial(g * per)
-        span(g - 1)
-        radial(g * per + 1)
-
-    span(ng - 1)
-    pending.extend([(wb.at[:, pl.ds(0, nz - 1)], w_send), (ysend.at[:, pl.ds(0, nr - 1)], y_send), (ya.at[pl.ds(0, nz - 1)], v_send.at[0])])
-    wait(yb.at[:, pl.ds(0, (nr - 1) * bi), :], y_recv)
-    for g in range(ng):
-        wait(ysend.at[0, 0], own_sem.at[2, g])
+    def owned_xy():
+        pending.append((ya.at[pl.ds(0, nz - 1)], v_send.at[0]))
+        wait(ya.at[pl.ds(0, nz - 1)], v_recv.at[0])
+        for g in range(ng):
+            wait(ysend.at[0, pl.ds(0, 2)], own_sem.at[3, g])
+        owned = yo.at[:, pl.ds(pl.multiple_of(m * pb, 8), pb), :]
+        pltpu.make_async_copy(ya.at[m // 2, :, m % 2], owned, in_sem.at[3]).start()
+        to_xy(lambda p: ya.at[p // 2, :, p % 2], owned, v_send.at[1], v_recv.at[1])
+        pending.append((yo.at[:, pl.ds(0, (nr - 1) * pb), :], v_send.at[1]))
+
+    def ring_owned_xy():
+        pltpu.make_async_copy(yz.at[m], yd.at[m], in_sem.at[4]).start()
+        to_xy(lambda p: yz.at[p], yd.at[m], v_send.at[2], v_recv.at[2])
+        pending.append((yd.at[pl.ds(0, nr - 1)], v_send.at[2]))
+
+    def ring_owned_z():
+        wait(yd.at[pl.ds(0, nr - 1)], v_recv.at[2])
+        wait(yd.at[0], in_sem.at[4])
+        owned = yo.at[:, pl.ds(pl.multiple_of(nr * pb + z * zb, 8), zb), :]
+        pltpu.make_async_copy(yd.at[pl.ds(2 * z, 2)], owned, in_sem.at[5]).start()
+        to_z(lambda p: yd.at[pl.ds(2 * p, 2)], owned, v_send.at[3], v_recv.at[3])
+        pending.append((yo.at[:, pl.ds(0, (nz - 1) * zb), :], v_send.at[3]))
+
+    def owned_end():
+        wait(yo.at[:, pl.ds(0, (nr - 1) * pb), :], v_recv.at[1])
+        wait(ya.at[0, :, 0], in_sem.at[3])
+        wait(yo.at[:, pl.ds(0, (nz - 1) * zb), :], v_recv.at[3])
+        wait(yd.at[pl.ds(0, 2)], in_sem.at[5])
 
     def chol_start(gram):
         ae[:, 0:LANES] = gram
@@ -286,17 +364,13 @@
     wait(sr.at[0], x_recv.at[0])
     part[0] = mm_nt(unfolded(), jnp.concatenate([sx[0, p] + sr[0, p] for p in range(2)], axis=1))
     reduce_1(0)
+    owned_z(0)
     yt[0] = yb[0].T
     reduce_2(0)
-    wait(ya.at[pl.ds(0, nz - 1)], v_recv.at[0])
-    for g in range(ng):
-        wait(ysend.at[0, pl.ds(0, 2)], own_sem.at[3, g])
-    owned = yo.at[:, pl.ds(pl.multiple_of(m * bi, 8), bi), :]
-    pltpu.make_async_copy(ya.at[m // 2, :, m % 2], owned, in_sem.at[3]).start()
-    to_xy(lambda p: ya.at[p // 2, :, p % 2], owned, v_send.at[1], v_recv.at[1])
-    pending.append((yo.at[:, pl.ds(0, (nr - 1) * bi), :], v_send.at[1]))
+    ring_owned_xy()
     yt[1] = yb[1].T
     reduce_3(0)
+    owned_z(1)
     reduce_end(0)
 
     sx[1] = mm(yt[...].reshape(2 * LANES, il), im[0]).reshape(2, LANES, LANES)
@@ -307,17 +381,16 @@
     wait(sr.at[1], x_recv.at[1])
     part[1] = mm(unfolded(), (sx[1] + sr[1]).reshape(2 * LANES, LANES))
     reduce_1(1)
+    owned_z(2)
     blocks = LANES // PIVOTS
     wait(gr.at[0], g_recv.at[0])
     chol_start(gx_s[0] + gr[0])
     chol_blocks(0, 3)
     reduce_2(1)
-    wait(yo.at[:, pl.ds(0, (nr - 1) * bi), :], v_recv.at[1])
-    wait(ya.at[0, :, 0], in_sem.at[3])
-    for q in range(2):
-        yot[q] = yo[q].T
+    owned_xy()
     chol_blocks(3, 6)
     reduce_3(1)
+    ring_owned_z()
     chol_blocks(6, blocks)
     linv[...] = ae[:, LANES:]
     reduce_end(1)
@@ -326,7 +399,8 @@
     to_core(gx_s.at[1], gr.at[1], g_send.at[1], g_recv.at[1])
     pending.append((gr.at[1], g_send.at[1]))
 
-    sx[2] = mm(yot[...].reshape(2 * LANES, il), images).reshape(2, LANES, LANES)
+    owned_end()
+    sx[2] = mm_tn(jnp.concatenate([yo[0], yo[1]], axis=1), images).reshape(2, LANES, LANES)
     exchange_begin(2)
     wait(gr.at[1], g_recv.at[1])
     chol_start(gx_s[1] + gr[1])
@@ -345,8 +419,10 @@
 
     def body(tensor, radial_factor, span_factor, start_factor):
         il = start_factor.shape[0]
+        pb = il // nr - il // nr // 4
+        zb = (il - nr * pb) // nz
+        nc, ng, nq, nh = pb // CHUNK, pb // GROUP, zb // CHUNK, zb // GROUP
         bi = il // nr
-        nc, ng = bi // CHUNK, bi // GROUP
         f32 = jnp.float32
         dma = pltpu.SemaphoreType.DMA
         vm = lambda *s: pltpu.VMEM(s, f32)
@@ -365,8 +441,10 @@
             vm(2, il, LANES),
             vm(2, LANES, LANES), vm(2, LANES, LANES),
             vm(LANES, 2 * LANES), vm(LANES, LANES),
-            vm(nz, 2, 2, bi, LANES), vm(2, il, LANES), vm(2, LANES, il),
-            dma((4,)), dma((4, nc)),
+            vm(nz, 2, 2, pb, LANES), vm(2, il, LANES), vm(nr, zb, LANES),
+            vm(nq, nz, CHUNK * 16, LANES), vm(nr * 8, nz * 32), vm(nz * 16, nr * 32),
+            vm(nr, zb * 4, LANES), vm(nr, zb * 4, LANES), vm(nz * 2, zb, LANES),
+            dma((6,)), dma((7, nc)),
             dma((2,)), dma((2,)),
             dma, dma((nc,)),
             dma, dma((nc,)),
@@ -374,7 +452,8 @@
             dma((3,)), dma((3,)),
             dma((2,)), dma((2,)),
             dma((2,)), dma((2,)), dma((2,)), dma((2,)), dma((2,)), dma((2,)),
-            dma((2,)), dma((2,)),
+            dma((4,)), dma((4,)),
+            dma((3,)), dma((nq + 1,)), dma((nh,)),
         ]
         rows = tensor.reshape(il * 16, LANES)
         hbm = pl.BlockSpec(memory_space=pltpu.HBM)

time: 122 us -> 113 us (0.926)
  Pallas kernels: 120 us -> 111 us
    pallas_call x1, Pallas kernels: 120 us -> 111 us  [body(): pl.pallas_call(functools.partial(kernel, nr, nz, gx), out_shape=jax.Shape...]
where the time goes in v5:
time: 113 us
  Pallas kernels  111 us (98%)
  local copies, waits for them, and re-layouts  1.57 us (1%)
    pallas_call x1, Pallas kernels, body(): pl.pallas_call(functools.partial(kernel, nr, nz, gx), out_shape=jax.Shape...  111 us

profile of v5, /device:TPU:1, one launch (start us, length us, event | category | flops | bytes accessed | tf_op | source)
XLA Modules:
  0.0 112.8 jit_solution(6915429920543213288)
XLA Ops:
  0.0 111.2 %shard_map.46 = f32[128,2,128]{2,1,0:T(2,128)} custom-call(f32[8192,128]{1,0:T(8,128)} %bitcast.4, f32[4,16]{1,0:T(4,128)} %a_ref.1, f32[4,16]{1,0:T(4,128)} %b_ref.1, f32[512,128]{1,0:T(8,128)} %f_ref.1), custom_call_target="tpu_custom_call" | custom-call | tf_op jit(solution)/shard_map/pallas_call | solution.py:460
  111.2 1.6 %copy.7 = f32[128,1,2,128]{3,2,1,0:T(2,128)} copy(f32[128,1,2,128]{3,2,1,0:T(2,128)} %bitcast.5) | data formatting | bytes 262144

commit v6 on v5

--- a/solution.py
+++ b/solution.py
@@ -118,25 +118,30 @@
     bg[z, 0:4, 0:rk] = bv[...]
     pl.semaphore_wait(barrier, (nr - 1) + (nz - 1) + 1)
 
+    def t_rows(peer, k):
+        return t_ref.at[pl.ds(pl.multiple_of((peer * pb + k * CHUNK) * 16, CHUNK * 16), CHUNK * 16), :]
+
+    def t_ring(peer, k):
+        return t_ref.at[pl.ds(pl.multiple_of((nr * pb + peer * zb + k * CHUNK) * 16, CHUNK * 16), CHUNK * 16), :]
+
+    def to_plane(k):
+        pltpu.make_async_copy(t_rows(m, k), xb.at[k, m], own_sem.at[0, k]).start()
+        to_xy(lambda p: t_rows(p, k), xb.at[k, m], t_send, t_recv.at[k])
+
+    def to_ring(k):
+        pltpu.make_async_copy(t_ring(z, k), xz.at[k, z], own_sem.at[4, k]).start()
+        to_z(lambda p: t_ring(p, k), xz.at[k, z], q_send.at[0], q_recv.at[k])
+
+    to_ring(0)
+    to_plane(0)
     to_xy(lambda p: ag.at[m], ag.at[m], ab_send.at[0], ab_recv.at[0])
     pending.append((ag.at[pl.ds(0, nr - 1)], ab_send.at[0]))
     to_z(lambda p: bg.at[z], bg.at[z], ab_send.at[1], ab_recv.at[1])
     pending.append((bg.at[pl.ds(0, nz - 1)], ab_send.at[1]))
 
-    def t_rows(peer, k):
-        return t_ref.at[pl.ds(pl.multiple_of((peer * pb + k * CHUNK) * 16, 64), CHUNK * 16), :]
-
-    def t_ring(peer, k):
-        return t_ref.at[pl.ds(pl.multiple_of((nr * pb + peer * zb + k * CHUNK) * 16, 64), CHUNK * 16), :]
-
-    def to_plane(k):
-        pltpu.make_async_copy(t_rows(m, k), xb.at[k, m], own_sem.at[0, k]).start()
-        to_xy(lambda p: t_rows(p, k), xb.at[k, m], t_send, t_recv.at[k], near_first)
-
-    @pl.loop(0, nq)
+    @pl.loop(1, nq)
     def _(k):
-        pltpu.make_async_copy(t_ring(z, k), xz.at[k, z], own_sem.at[4, k]).start()
-        to_z(lambda p: t_ring(p, k), xz.at[k, z], q_send.at[0], q_recv.at[k])
+        to_ring(k)
         to_plane(k)
 
     @pl.loop(nq, nc)
@@ -170,18 +175,16 @@
         wait(xb.at[k, pl.ds(0, nr - 1)], t_recv.at[k])
         wait(xb.at[k, 0], own_sem.at[0, k])
 
-        @pl.loop(0, CHUNK // 2)
-        def _(h):
-            at = pl.multiple_of(h * 32, 32)
-            both = xb[k, :, pl.ds(at, 32), :]
+        for h in range(CHUNK // 2):
+            both = xb[k, :, pl.ds(h * 32, 32), :]
             x0 = both[:, 0:16, :].reshape(nr * 16, LANES)
             x1 = both[:, 16:32, :].reshape(nr * 16, LANES)
             u = mm(ma[...], jnp.concatenate([x0, x1], axis=1))
-            at8 = pl.multiple_of((k % per) * CHUNK * 8 + h * 16, 16)
-            ub[k // per, :, pl.ds(at8, 8), :] = u[:, 0:LANES].reshape(nz, 8, LANES)
-            ub[k // per, :, pl.ds(at8 + 8, 8), :] = u[:, LANES:].reshape(nz, 8, LANES)
-
-        g, half = k // per, pl.ds(pl.multiple_of((k % per) * CHUNK * 8, CHUNK * 8), CHUNK * 8)
+            at = (k % per) * CHUNK * 8 + h * 16
+            ub[k // per, :, pl.ds(at, 8), :] = u[:, 0:LANES].reshape(nz, 8, LANES)
+            ub[k // per, :, pl.ds(at + 8, 8), :] = u[:, LANES:].reshape(nz, 8, LANES)
+
+        g, half = k // per, pl.ds((k % per) * CHUNK * 8, CHUNK * 8)
         pltpu.make_async_copy(ub.at[g, z, half], wb.at[g, z, half], own_sem.at[1, k]).start()
         to_z(lambda p: ub.at[g, p, half], wb.at[g, z, half], w_send, w_recv.at[k])
 
@@ -202,7 +205,7 @@
         wait(xz.at[k, 0], own_sem.at[4, k])
         for h in range(CHUNK // 2):
             rows = xz[k, :, pl.ds(h * 32, 32), :].reshape(nz * 32, LANES)
-            vs[:, pl.ds((k * 2 + h) * 8, 8), :] = mm(zm[...], rows).reshape(nr, 8, LANES)
+            vs[:, pl.ds((k * (CHUNK // 2) + h) * 8, 8), :] = mm(zm[...], rows).reshape(nr, 8, LANES)
         if k % per == per - 1:
             rows = pl.ds((k // per) * GROUP * 4, GROUP * 4)
             pltpu.make_async_copy(vs.at[m, rows], vr.at[m, rows], own_sem.at[5, k // per]).start()
@@ -220,21 +223,19 @@
         pltpu.make_async_copy(yz.at[pl.ds(2 * z, 2), part_rows], ring_y(g), own_sem.at[6, g]).start()
         to_z(lambda p: yz.at[pl.ds(2 * p, 2), part_rows], ring_y(g), q_send.at[2], q_recv.at[nq])
 
-    radial(0)
-    radial(1)
-    ring_span(0)
-    radial(2)
-    span(0)
-    ring_span(1)
-    radial(3)
-    ring_span(2)
-    radial(4)
-    span(1)
-    ring_span(3)
-    radial(5)
+    spans = rings = 0
+    for k in range(nc):
+        radial(k)
+        if k % per == per // 2 and k > per:
+            span(spans)
+            spans += 1
+        while rings < nq and rings * (nc - 1) < k * nq:
+            ring_span(rings)
+            rings += 1
     ring_radial(0)
-    span(2)
-    ring_radial(1)
+    span(ng - 1)
+    for g in range(1, zb // GROUP):
+        ring_radial(g)
     pending.extend([(wb.at[:, pl.ds(0, nz - 1)], w_send), (ysend.at[:, pl.ds(0, nr - 1)], y_send)])
     pending.extend([(vr.at[pl.ds(0, nr - 1)], q_send.at[1]), (yb.at[:, pl.ds(0, (nz - 1) * zb), :], q_send.at[2])])
     wait(yb.at[:, pl.ds(0, (nr - 1) * pb), :], y_recv)
@@ -325,8 +326,12 @@
         to_core(sx.at[n], sr.at[n], x_send.at[n], x_recv.at[n])
         pending.append((sr.at[n], x_send.at[n]))
 
-    def reduce_1(n):
-        to_xy(lambda p: part.at[n, pl.ds(pl.multiple_of(p * bi, 8), bi), :], r1.at[n, m], r1_send.at[n], r1_recv.at[n])
+    def reduce_1(n, product):
+        for dy in sorted(range(gy), key=lambda d: -min(d, gy - d)):
+            block = pl.ds(pl.multiple_of(ys[dy] * bi, 8), gx * bi)
+            part[n, block, :] = product(jnp.concatenate([yb[0, block, :], yb[1, block, :]], axis=1))
+            peers = [ys[dy] + xs[dx] for dx in sorted(range(gx), key=lambda d: -min(d, gx - d)) if dx or dy]
+            to_xy(lambda p: part.at[n, pl.ds(pl.multiple_of(p * bi, 8), bi), :], r1.at[n, m], r1_send.at[n], r1_recv.at[n], peers)
         pending.append((r1.at[n, pl.ds(0, nr - 1)], r1_send.at[n]))
         r1[n, m] = part[n, pl.ds(pl.multiple_of(m * bi, 8), bi), :]
 
@@ -362,8 +367,8 @@
         sx[0, p] = both[:, p * LANES:(p + 1) * LANES]
     exchange_begin(0)
     wait(sr.at[0], x_recv.at[0])
-    part[0] = mm_nt(unfolded(), jnp.concatenate([sx[0, p] + sr[0, p] for p in range(2)], axis=1))
-    reduce_1(0)
+    small = jnp.concatenate([sx[0, p] + sr[0, p] for p in range(2)], axis=1)
+    reduce_1(0, lambda rows: mm_nt(rows, small))
     owned_z(0)
     yt[0] = yb[0].T
     reduce_2(0)
@@ -379,8 +384,8 @@
     to_core(gx_s.at[0], gr.at[0], g_send.at[0], g_recv.at[0])
     pending.append((gr.at[0], g_send.at[0]))
     wait(sr.at[1], x_recv.at[1])
-    part[1] = mm(unfolded(), (sx[1] + sr[1]).reshape(2 * LANES, LANES))
-    reduce_1(1)
+    small = (sx[1] + sr[1]).reshape(2 * LANES, LANES)
+    reduce_1(1, lambda rows: mm(rows, small))
     owned_z(2)
     blocks = LANES // PIVOTS
     wait(gr.at[0], g_recv.at[0])

time: 113 us -> 110 us (0.973)
  Pallas kernels: 111 us -> 109 us
    pallas_call x1, Pallas kernels: 111 us -> 109 us  [body(): pl.pallas_call(functools.partial(kernel, nr, nz, gx), out_shape=jax.Shape...]
where the time goes in v6:
time: 110 us
  Pallas kernels  109 us (99%)
  local copies, waits for them, and re-layouts  1.57 us (1%)
    pallas_call x1, Pallas kernels, body(): pl.pallas_call(functools.partial(kernel, nr, nz, gx), out_shape=jax.Shape...  109 us

profile of v6, /device:TPU:1, one launch (start us, length us, event | category | flops | bytes accessed | tf_op | source)
XLA Modules:
  0.0 110.3 jit_solution(1524773585474342972)
XLA Ops:
  0.0 108.7 %shard_map.46 = f32[128,2,128]{2,1,0:T(2,128)} custom-call(f32[8192,128]{1,0:T(8,128)} %bitcast.4, f32[4,16]{1,0:T(4,128)} %a_ref.1, f32[4,16]{1,0:T(4,128)} %b_ref.1, f32[512,128]{1,0:T(8,128)} %f_ref.1), custom_call_target="tpu_custom_call" | custom-call | tf_op jit(solution)/shard_map/pallas_call | solution.py:465
  108.7 1.6 %copy.7 = f32[128,1,2,128]{3,2,1,0:T(2,128)} copy(f32[128,1,2,128]{3,2,1,0:T(2,128)} %bitcast.5) | data formatting | bytes 262144

commit v7 on v6

--- a/solution.py
+++ b/solution.py
@@ -12,7 +12,7 @@
 LANES = 128
 CHUNK = 4
 GROUP = 8
-PIVOTS = 16
+PIVOTS = 32
 
 
 def mm(a, b):
@@ -32,6 +32,18 @@
     rest = x - high.astype(jnp.float32)
     mid = rest.astype(jnp.bfloat16)
     return high, mid, (rest - mid.astype(jnp.float32)).astype(jnp.bfloat16)
+
+
+def split2(x):
+    high = x.astype(jnp.bfloat16)
+    return high, (x - high.astype(jnp.float32)).astype(jnp.bfloat16)
+
+
+def mm3(a, b, dims=((1,), (0,))):
+    ah, al = split2(a)
+    bh, bl = split2(b)
+    one = lambda x, y: lax.dot_general(x, y, (dims, ((), ())), preferred_element_type=jnp.float32)
+    return one(ah, bh) + (one(ah, bl) + one(al, bh))
 
 
 def mm_tn_stacked(a, b):
@@ -179,7 +191,7 @@
             both = xb[k, :, pl.ds(h * 32, 32), :]
             x0 = both[:, 0:16, :].reshape(nr * 16, LANES)
             x1 = both[:, 16:32, :].reshape(nr * 16, LANES)
-            u = mm(ma[...], jnp.concatenate([x0, x1], axis=1))
+            u = mm3(ma[...], jnp.concatenate([x0, x1], axis=1))
             at = (k % per) * CHUNK * 8 + h * 16
             ub[k // per, :, pl.ds(at, 8), :] = u[:, 0:LANES].reshape(nz, 8, LANES)
             ub[k // per, :, pl.ds(at + 8, 8), :] = u[:, LANES:].reshape(nz, 8, LANES)
@@ -195,7 +207,7 @@
         for h in range(per):
             wait(wb.at[g, pl.ds(0, nz - 1), pl.ds(0, CHUNK * 8)], w_recv.at[g * per + h])
             wait(wb.at[g, 0, pl.ds(0, CHUNK * 8)], own_sem.at[1, g * per + h])
-        y = mm(mb[...], wb[g].reshape(nz * 64, LANES))
+        y = mm3(mb[...], wb[g].reshape(nz * 64, LANES))
         ysend[g] = y.reshape(nr, 2, GROUP, LANES)
         pltpu.make_async_copy(ysend.at[g, m], y_rows(g), own_sem.at[2, g]).start()
         to_xy(lambda p: ysend.at[g, p], y_rows(g), y_send, y_recv)
@@ -205,7 +217,7 @@
         wait(xz.at[k, 0], own_sem.at[4, k])
         for h in range(CHUNK // 2):
             rows = xz[k, :, pl.ds(h * 32, 32), :].reshape(nz * 32, LANES)
-            vs[:, pl.ds((k * (CHUNK // 2) + h) * 8, 8), :] = mm(zm[...], rows).reshape(nr, 8, LANES)
+            vs[:, pl.ds((k * (CHUNK // 2) + h) * 8, 8), :] = mm3(zm[...], rows).reshape(nr, 8, LANES)
         if k % per == per - 1:
             rows = pl.ds((k // per) * GROUP * 4, GROUP * 4)
             pltpu.make_async_copy(vs.at[m, rows], vr.at[m, rows], own_sem.at[5, k // per]).start()
@@ -218,7 +230,7 @@
         rows, part_rows = pl.ds(g * GROUP * 4, GROUP * 4), pl.ds(g * GROUP, GROUP)
         wait(vr.at[pl.ds(0, nr - 1), rows], u_recv.at[g])
         wait(vr.at[0, rows], own_sem.at[5, g])
-        y = mm(rm[...], vr[:, rows, :].reshape(nr * 32, LANES))
+        y = mm3(rm[...], vr[:, rows, :].reshape(nr * 32, LANES))
         yz[:, part_rows, :] = y.reshape(rj, GROUP, LANES)
         pltpu.make_async_copy(yz.at[pl.ds(2 * z, 2), part_rows], ring_y(g), own_sem.at[6, g]).start()
         to_z(lambda p: yz.at[pl.ds(2 * p, 2), part_rows], ring_y(g), q_send.at[2], q_recv.at[nq])
@@ -362,13 +374,13 @@
     def unfolded():
         return jnp.concatenate([yb[0], yb[1]], axis=1)
 
-    both = mm(f0t[...], unfolded())
+    both = mm3(f0t[...], unfolded())
     for p in range(2):
         sx[0, p] = both[:, p * LANES:(p + 1) * LANES]
     exchange_begin(0)
     wait(sr.at[0], x_recv.at[0])
     small = jnp.concatenate([sx[0, p] + sr[0, p] for p in range(2)], axis=1)
-    reduce_1(0, lambda rows: mm_nt(rows, small))
+    reduce_1(0, lambda rows: mm3(rows, small, ((1,), (1,))))
     owned_z(0)
     yt[0] = yb[0].T
     reduce_2(0)
@@ -378,25 +390,25 @@
     owned_z(1)
     reduce_end(0)
 
-    sx[1] = mm(yt[...].reshape(2 * LANES, il), im[0]).reshape(2, LANES, LANES)
+    sx[1] = mm3(yt[...].reshape(2 * LANES, il), im[0]).reshape(2, LANES, LANES)
     exchange_begin(1)
     gx_s[0] = mm_tn(im[0], im[0])
     to_core(gx_s.at[0], gr.at[0], g_send.at[0], g_recv.at[0])
     pending.append((gr.at[0], g_send.at[0]))
     wait(sr.at[1], x_recv.at[1])
     small = (sx[1] + sr[1]).reshape(2 * LANES, LANES)
-    reduce_1(1, lambda rows: mm(rows, small))
+    reduce_1(1, lambda rows: mm3(rows, small))
     owned_z(2)
     blocks = LANES // PIVOTS
     wait(gr.at[0], g_recv.at[0])
     chol_start(gx_s[0] + gr[0])
-    chol_blocks(0, 3)
+    chol_blocks(0, 1)
     reduce_2(1)
     owned_xy()
-    chol_blocks(3, 6)
+    chol_blocks(1, 3)
     reduce_3(1)
     ring_owned_z()
-    chol_blocks(6, blocks)
+    chol_blocks(3, blocks)
     linv[...] = ae[:, LANES:]
     reduce_end(1)
     images = mm_nt(im[1], linv[...])
@@ -411,8 +423,9 @@
     chol_start(gx_s[1] + gr[1])
     chol_blocks(0, blocks)
     wait(sr.at[2], x_recv.at[2])
+    core = mm_nt(ae[:, LANES:], (sx[2] + sr[2]).reshape(2 * LANES, LANES))
     for q in range(2):
-        out_ref[:, q, :] = mm_nt(ae[:, LANES:], sx[2, q] + sr[2, q])
+        out_ref[:, q, :] = core[:, q * LANES:(q + 1) * LANES]
     finish()
 
 

time: 110 us -> 108 us (0.982)
  Pallas kernels: 109 us -> 106 us
    pallas_call x1, Pallas kernels: 109 us -> 106 us  [body(): pl.pallas_call(functools.partial(kernel, nr, nz, gx), out_shape=jax.Shape...]
where the time goes in v7:
time: 108 us
  Pallas kernels  106 us (98%)
  local copies, waits for them, and re-layouts  1.57 us (1%)
    pallas_call x1, Pallas kernels, body(): pl.pallas_call(functools.partial(kernel, nr, nz, gx), out_shape=jax.Shape...  106 us

profile of v7, /device:TPU:1, one launch (start us, length us, event | category | flops | bytes accessed | tf_op | source)
XLA Modules:
  0.0 107.9 jit_solution(6794921383196014995)
XLA Ops:
  0.0 106.3 %shard_map.46 = f32[128,2,128]{2,1,0:T(2,128)} custom-call(f32[8192,128]{1,0:T(8,128)} %bitcast.4, f32[4,16]{1,0:T(4,128)} %a_ref.1, f32[4,16]{1,0:T(4,128)} %b_ref.1, f32[512,128]{1,0:T(8,128)} %f_ref.1), custom_call_target="tpu_custom_call" | custom-call | tf_op jit(solution)/shard_map/pallas_call | solution.py:478
  106.3 1.6 %copy.7 = f32[128,1,2,128]{3,2,1,0:T(2,128)} copy(f32[128,1,2,128]{3,2,1,0:T(2,128)} %bitcast.5) | data formatting | bytes 262144
